TPU v7x, 128 devices: a whole 4x4x4 slice. The times are simulated.
128 devices in a mesh: rep: 4 (over z), fsdp: 32 (over x, y, core).
Axes of the slice: x: 4, y: 4, z: 4, core: 2. Of those that a mesh axis runs over, the one named last changes fastest.
Arguments:
- momentum: float32 [4, 3, 2048, 8192], P('rep', None, 'fsdp'), may hold values from -43 to 43, as said below
- gradient: float32 [4, 3, 2048, 8192], P('rep', None, 'fsdp'), may hold values from -6 to 6
- basis: float32 [8192, 384], P(('rep', 'fsdp')), may hold values from -1 to 1
Outputs:
- momentum_next: float32 [4, 3, 2048, 8192], P('rep', None, 'fsdp')
- update: float32 [3, 2048, 8192], P(None, 'fsdp')
- basis_next: float32 [8192, 384], P(('rep', 'fsdp'))
Inputs may be any that keep to these rules, and one draw needn't show every extreme that they name: momentum of each replica group, rows and columns with different scales.
All inputs are finite; a program needn't handle non-finite values.
Results may differ from a plain program's by a relative error of at most 0.0003.
Values sent between devices are 32-bit elements; how exact they have to be, the bound alone decides.
A program may use at most 192 MiB of HBM per device.

v0:
```python
import jax
import jax.numpy as jnp
from jax import lax
from jax.sharding import PartitionSpec as P

RANK = 128


HIGH = lax.Precision.HIGHEST


def body(momentum, gradient, basis):
    blend = momentum[0] + gradient[0]
    rows = blend.shape[1]
    width = blend.shape[2]
    n_rep = lax.axis_size("rep")
    n_fsdp = lax.axis_size("fsdp")
    rows_all = rows * n_fsdp
    shard_rows = basis.shape[0]
    gain = jnp.sqrt(jnp.float32(rows_all * width / RANK))
    piece = lax.all_gather(basis, ("rep", "fsdp"), axis=0, tiled=True)
    columns = blend
    right = piece.reshape(piece.shape[0], 3, RANK)
    local = jnp.einsum("krc,cks->krs", columns, right, precision=HIGH)
    projected = lax.psum(local, "rep") / n_rep
    for sweep in range(2):
        gram = jnp.einsum("krs,krt->kst", projected, projected, precision=HIGH)
        gram = lax.psum(gram, "fsdp")
        lower = jnp.linalg.cholesky(gram)
        solved = jax.scipy.linalg.solve_triangular(
            lower, jnp.transpose(projected, (0, 2, 1)), lower=True
        )
        projected = jnp.transpose(solved, (0, 2, 1))
    columns = blend
    term = jnp.einsum("krc,krs->cks", columns, projected, precision=HIGH)
    shard = (
        lax.psum_scatter(
            term.reshape(lax.axis_size(("rep", "fsdp")) * shard_rows, 3 * RANK),
            ("rep", "fsdp"),
            scatter_dimension=0,
            tiled=True,
        )
        / n_rep
    )
    sums = lax.psum(jnp.sum(shard * shard, axis=0), ("rep", "fsdp"))
    scales = 1.0 / jnp.sqrt(sums + 1e-06)
    basis_next = shard * scales
    piece = lax.all_gather(shard, ("rep", "fsdp"), axis=0, tiled=True)
    count = piece.shape[0]
    columns = blend
    term = piece.reshape(count, 3, RANK)
    normed = (piece * scales).reshape(count, 3, RANK)
    feedback = jnp.einsum("krs,cks->krc", projected, term, precision=HIGH)
    steered = gain * jnp.einsum("krs,cks->krc", projected, normed, precision=HIGH)
    results = jnp.stack([columns - 0.05 * feedback, steered])
    return (results[0][None], results[1], basis_next)


def solution(mesh):
    placed = (P("rep", None, "fsdp", None), P("rep", None, "fsdp", None), P(("rep", "fsdp"), None))
    return jax.shard_map(
        body,
        mesh=mesh,
        in_specs=placed,
        out_specs=(P("rep", None, "fsdp", None), P(None, "fsdp", None), P(("rep", "fsdp"), None)),
        check_vma=False,
    )
```

profile of v0, /device:TPU:1, one launch (start us, length us, event | category | flops | bytes accessed | tf_op | source)
XLA Modules:
  0.0 939.3 jit_solution(16066230203173743581)
XLA Ops:
  7.9 80.2 %all-gather.3.cloned.1.call-done = f32[8192,384]{1,0:T(8,128)} async-done(((f32[64,384]{1,0:T(8,128)}), f32[8192,384]{1,0:T(8,128)}) %all-gather.3.cloned.1.call-update) | async-done | bytes 12582928 | tf_op jit(solution)/shard_map/all_gather | solution.py:21
  88.1 12.5 %copy.39 = f32[8192,384]{0,1:T(8,128)} copy(f32[8192,384]{1,0:T(8,128)} %all-gather.3.cloned.1.call-done) | data formatting | bytes 25165824 | tf_op jit(solution)/shard_map/all_gather | solution.py:21
  100.6 18.5 %fusion.4 = f32[3,64,128]{2,1,0:T(8,128)} fusion(f32[8192,3,128]{0,2,1:T(8,128)} %bitcast.47, f32[1,3,64,8192]{3,2,1,0:T(8,128)} %param.6, f32[1,3,64,8192]{3,2,1,0:T(8,128)} %param.7), kind=kOutput, calls=%fused_computation.6 | convolution fusion | flops 2417491968 | bytes 25264128 | tf_op jit(solution)/shard_map/krc,cks->krs/dot_general | solution.py:24
  119.2 38.4 %all-reduce.4.cloned.1.call-done = f32[3,64,128]{2,1,0:T(8,128)} async-done(((f32[3,64,128]{2,1,0:T(8,128)}), f32[3,64,128]{2,1,0:T(8,128)}) %all-reduce.4.cloned.1.call-update) | async-done | bytes 98320 | tf_op jit(solution)/shard_map/psum | solution.py:25
  157.6 2.1 fusion.14
  160.1 103.0 %all-reduce.6.cloned.1.call-done = f32[3,128,128]{1,2,0:T(8,128)} async-done(((f32[3,128,128]{1,2,0:T(8,128)}), f32[3,128,128]{1,2,0:T(8,128)}) %all-reduce.6.cloned.1.call-update) | async-done | bytes 196624 | tf_op jit(solution)/shard_map/psum | solution.py:28
  263.0 1.1 copy.42
  265.1 35.2 %custom-call.8 = f32[3,128,128]{2,1,0:T(8,128)S(1)} custom-call(f32[3,128,128]{2,1,0:T(8,128)S(1)} %fusion.11), custom_call_target="Cholesky" | custom-call | tf_op jit(solution)/shard_map/jit(cholesky)/cholesky | solution.py:29
  300.5 29.5 %custom-call.9 = f32[3,1,128,128]{2,3,1,0:T(8,128)S(1)} custom-call(f32[3,1,128,128]{3,2,1,0:T(8,128)S(1)} %select_bitcast_fusion.1), custom_call_target="InvertDiagBlocksLowerTriangular" | custom-call | tf_op jit(solution)/shard_map/jit(_solve_triangular)/vmap()/triangular_solve | solution.py:30
  330.0 1.2 fusion.9
  331.2 1.2 fusion.22
  332.4 98.4 %all-reduce.8.cloned.1.call-done = f32[3,128,128]{1,2,0:T(8,128)} async-done(((f32[3,128,128]{1,2,0:T(8,128)}), f32[3,128,128]{1,2,0:T(8,128)}) %all-reduce.8.cloned.1.call-update) | async-done | bytes 196624 | tf_op jit(solution)/shard_map/psum | solution.py:28
  430.9 1.1 copy.45
  432.9 35.4 %custom-call.10 = f32[3,128,128]{2,1,0:T(8,128)S(1)} custom-call(f32[3,128,128]{2,1,0:T(8,128)S(1)} %fusion.8), custom_call_target="Cholesky" | custom-call | tf_op jit(solution)/shard_map/jit(cholesky)/cholesky | solution.py:29
  468.5 29.5 %custom-call.11 = f32[3,1,128,128]{2,3,1,0:T(8,128)S(1)} custom-call(f32[3,1,128,128]{3,2,1,0:T(8,128)S(1)} %select_bitcast_fusion), custom_call_target="InvertDiagBlocksLowerTriangular" | custom-call | tf_op jit(solution)/shard_map/jit(_solve_triangular)/vmap()/triangular_solve | solution.py:30
  498.3 15.7 %fusion.2 = f32[3,128,8192]{2,1,0:T(8,128)} fusion(f32[3,128,64]{1,2,0:T(8,128)S(1)} %fusion.6, f32[1,3,64,8192]{3,2,1,0:T(8,128)} %param.6, f32[1,3,64,8192]{3,2,1,0:T(8,128)} %param.7), kind=kOutput, calls=%fused_computation.4 | convolution fusion | flops 2417491968 | bytes 25264128 | tf_op jit(solution)/shard_map/krc,krs->cks/dot_general | solution.py:35
  514.1 12.6 %copy.60 = f32[8192,384]{1,0:T(8,128)} copy(f32[8192,384]{0,1:T(8,128)} %bitcast.48) | data formatting | bytes 25165824
  527.0 219.3 %reduce-scatter.4.cloned.1.call-done = f32[64,384]{1,0:T(8,128)} async-done(((f32[8192,384]{1,0:T(8,128)}), f32[64,384]{1,0:T(8,128)}) %reduce-scatter.4.cloned.1.call-update) | async-done | bytes 98320
  747.4 64.3 %psum.31 = f32[384]{0:T(512)S(1)} all-reduce(f32[384]{0:T(512)S(1)} %multiply_reduce_fusion), channel_id=1, replica_groups=mesh['rep'=4,'fsdp'=32] {'rep','fsdp'}, use_global_device_ids=true, to_apply=%region_7.10 | all-reduce | flops 384 | bytes 3072 | tf_op jit(solution)/shard_map/psum | solution.py:45
  813.4 69.5 %all-gather.5.cloned.1.call-done = f32[8192,384]{1,0:T(8,128)} async-done(((f32[64,384]{1,0:T(8,128)}), f32[8192,384]{1,0:T(8,128)}) %all-gather.5.cloned.1.call-update) | async-done | bytes 12582928 | tf_op jit(solution)/shard_map/all_gather | solution.py:48
  882.9 12.5 %copy.48 = f32[8192,384]{0,1:T(8,128)} copy(f32[8192,384]{1,0:T(8,128)} %all-gather.5.cloned.1.call-done) | data formatting | bytes 25165824 | tf_op jit(solution)/shard_map/all_gather | solution.py:48
  895.5 14.2 %fusion.1 = f32[1,3,64,8192]{3,2,1,0:T(8,128)} fusion(f32[3,128,64]{1,2,0:T(8,128)S(1)} %fusion.6, f32[8192,3,128]{0,2,1:T(8,128)} %bitcast.45, f32[1,3,64,8192]{3,2,1,0:T(8,128)} %param.6, f32[1,3,64,8192]{3,2,1,0:T(8,128)} %param.7), kind=kOutput, calls=%fused_computation.3 | convolution fusion | flops 2420637696 | bytes 31555584 | tf_op jit(solution)/shard_map/krs,cks->krc/dot_general | solution.py:53
  909.7 11.2 %broadcast_multiply_fusion = f32[8192,384]{0,1:T(8,128)} fusion(f32[8192,384]{0,1:T(8,128)} %copy.48, f32[384]{0:T(512)S(1)} %get-tuple-element.17), kind=kLoop, calls=%fused_computation.8 | loop fusion | flops 3145728 | bytes 25167360 | tf_op jit(solution)/shard_map/mul | solution.py:52
  920.9 11.6 %convolution_multiply_fusion = f32[3,64,8192]{2,1,0:T(8,128)} fusion(f32[3,128,64]{1,2,0:T(8,128)S(1)} %fusion.6, f32[8192,3,128]{0,2,1:T(8,128)} %bitcast.46), kind=kOutput, calls=%fused_computation | convolution fusion | flops 2417491968 | bytes 18972672 | tf_op jit(solution)/shard_map/krs,cks->krc/dot_general | solution.py:54
  (29 shorter events, 7.0 us)
Async XLA Ops:
  7.2 80.9 %all-gather.3.cloned.1.call-start = ((), (), s32[]{:S(2)}) async-start(), calls=%async_computation.1 | async-start | bytes 12681216 | tf_op jit(solution)/shard_map/all_gather | solution.py:21
  7.9 149.7 %all-reduce.4.cloned.1.call-start = ((), (), s32[]{:S(2)}) async-start(), calls=%async_computation.2 | async-start | bytes 196608 | tf_op jit(solution)/shard_map/psum | solution.py:25
  119.1 143.9 %all-reduce.6.cloned.1.call-start = ((), (), s32[]{:S(2)}) async-start(), calls=%async_computation.3 | async-start | bytes 393216 | tf_op jit(solution)/shard_map/psum | solution.py:28
  159.8 271.1 %all-reduce.8.cloned.1.call-start = ((), (), s32[]{:S(2)}) async-start(), calls=%async_computation.4 | async-start | bytes 393216 | tf_op jit(solution)/shard_map/psum | solution.py:28
  332.4 413.8 %reduce-scatter.4.cloned.1.call-start = ((), (), s32[]{:S(2)}) async-start(), calls=%async_computation.6 | async-start | bytes 12681216
  526.7 356.3 %all-gather.5.cloned.1.call-start = ((), (), s32[]{:S(2)}) async-start(), calls=%async_computation.5 | async-start | bytes 12681216 | tf_op jit(solution)/shard_map/all_gather | solution.py:48
Sparse Core Ops, SparseCore 0:
  11.1 76.9 all-gather.2
  119.3 38.3 all-reduce.3
  161.8 101.1 all-reduce.5
  332.5 98.3 all-reduce.7
  526.8 219.4 reduce-scatter.3
  812.8 70.1 all-gather.4
where the time goes:
time: 940 us; the launch traced here: 939 us
  waiting for transfers between devices  610 us (65%)
  other arithmetic  143 us (15%)
  matrix products  64.8 us (7%)
  blocking collectives  64.3 us (7%)
  local copies, waits for them, and re-layouts  42.3 us (4%)
  between operations  14.2 us (2%)
    unnamed x7, waiting for transfers between devices  220 us
    psum x2, waiting for transfers between devices, body(): gram = lax.psum(gram, 'fsdp')  201 us
    all_gather x1, waiting for transfers between devices, body(): piece = lax.all_gather(basis, ('rep', 'fsdp'), axis=0, tiled=True)  80.2 us
    another operation x7, other arithmetic, body(): lower = jnp.linalg.cholesky(gram)  70.9 us
    all_gather x1, waiting for transfers between devices, body(): piece = lax.all_gather(shard, ('rep', 'fsdp'), axis=0, tiled=True)  69.5 us
    psum x1, blocking collectives, body(): sums = lax.psum(jnp.sum(shard * shard, axis=0), ('rep', 'fsdp'))  64.3 us
    another operation x5, other arithmetic, body(): jax.scipy.linalg.solve_triangular(lower, jnp.transpose(projected, (0, 2,...  59.2 us
    psum x1, waiting for transfers between devices, body(): projected = lax.psum(local, 'rep') / n_rep  38.4 us
  transfers between devices with their start and end apart: 6, of which 6 were waited for; matrix products, arithmetic and copies ran while one was open for 0% of the time, Pallas kernels for 0%

commit v1 on v0

v1 whole, which is shorter than its diff:
```python
import functools

import jax
import jax.numpy as jnp
from jax import lax
from jax.experimental import pallas as pl
from jax.experimental.pallas import tpu as pltpu
from jax.sharding import PartitionSpec as P

MESH = pl.DeviceIdType.MESH
HIGH = lax.Precision.HIGHEST
F32 = jnp.float32
BF16 = jnp.bfloat16
RANK = 128
N = 4
OFF = (0, 1, 3, 2)
ANY = pl.BlockSpec(memory_space=pl.ANY)
VMEM = pl.BlockSpec(memory_space=pltpu.VMEM)


def axis_of(third, phase):
    return (2, 1, 0)[(third + phase) % 3]


class Place:
    def __init__(self):
        self.rep = lax.axis_index("rep")
        self.fsdp = lax.axis_index("fsdp")
        self.core = lax.rem(self.fsdp, 2)
        self.at = (self.rep, lax.div(self.fsdp, 8), lax.rem(lax.div(self.fsdp, 2), N))

    def far(self, axis, distance):
        if isinstance(distance, int) and distance == 0:
            return self.at[axis]
        return lax.rem(self.at[axis] + distance, N)

    def chip(self, axis, distance):
        at = list(self.at)
        at[axis] = self.far(axis, distance)
        return (at[0], (at[1] * N + at[2]) * 2 + self.core)

    def sibling(self):
        return (self.rep, self.fsdp + 1 - 2 * self.core)

    def line(self, third, j1, j2, i):
        off1, off2 = dyn_off(j1), dyn_off(j2)
        places = []
        for t in range(3):
            where = [None] * 3
            where[axis_of(t, 0)] = i
            where[axis_of(t, 1)] = self.far(axis_of(t, 1), off1)
            where[axis_of(t, 2)] = self.far(axis_of(t, 2), off2)
            places.append(where)
        return [jnp.where(third == 0, a, jnp.where(third == 1, b, c)) for a, b, c in zip(*places)]


def dyn_off(j):
    return OFF[j] if isinstance(j, int) else j + (j // 2) * (5 - 2 * j)


def greet(place, distances):
    barrier = pltpu.get_barrier_semaphore()
    peers = [place.sibling()] + [place.chip(axis, d) for axis, d in distances]
    for peer in peers:
        pl.semaphore_signal(barrier, inc=1, device_id=peer, device_id_type=MESH)
    pl.semaphore_wait(barrier, len(peers))


NEAR = [(axis, d) for axis in range(3) for d in (1, 3)]


def gather_sems():
    dma = pltpu.SemaphoreType.DMA
    return [dma((3, 3, 4, 2))] * 4 + [dma((3, 4, 4))] * 2


def gather(place, buf, sems, hook=None):
    send_a, recv_a, send_b, recv_b, send_d, recv_d = sems
    core = place.core
    rows = buf.shape[5]
    half = rows // 2

    def index(t, p, j, da, part=None):
        where = [None] * 3
        for q in range(3):
            axis = axis_of(t, q)
            if q < p - 1:
                where[axis] = slice(None)
            elif q == p - 1:
                where[axis] = place.far(axis, dyn_off(j))
            elif q == p:
                where[axis] = place.far(axis, da)
            else:
                where[axis] = place.at[axis]
        span = slice(None) if part is None else pl.ds(part * half, half)
        return (t, *where, core, span)

    def copy_a(t, p, j, d, da):
        spot = buf.at[index(t, p, j, da)]
        return pltpu.make_async_remote_copy(
            spot, spot, send_a.at[t, p, j, d], recv_a.at[t, p, j, d],
            device_id=place.chip(axis_of(t, p), 1 if d == 0 else 3), device_id_type=MESH)

    def copy_b(t, p, j, d, da):
        spot = buf.at[index(t, p, j, da, d)]
        return pltpu.make_async_remote_copy(
            spot, spot, send_b.at[t, p, j, d], recv_b.at[t, p, j, d],
            device_id=place.chip(axis_of(t, p), 1 if d == 0 else 3), device_id_type=MESH)

    def copy_d(t, j1, j2, whose):
        where = [None] * 3
        where[axis_of(t, 0)] = slice(None)
        where[axis_of(t, 1)] = place.far(axis_of(t, 1), dyn_off(j1))
        where[axis_of(t, 2)] = place.far(axis_of(t, 2), dyn_off(j2))
        spot = buf.at[(t, *where, whose)]
        return pltpu.make_async_remote_copy(
            spot, spot, send_d.at[t, j1, j2], recv_d.at[t, j1, j2],
            device_id=place.sibling(), device_id_type=MESH)

    def start_a(t, p, j):
        for d in range(2):
            copy_a(t, p, j, d, 0).start()

    def land_a(t, p, j, d):
        copy_a(t, p, j, d, 3 if d == 0 else 1).wait_recv()
        copy_b(t, p, j, d, 3 if d == 0 else 1).start()

    def land_b(t, p, j):
        for d in range(2):
            copy_b(t, p, j, d, 2).wait_recv()

    def line_done(j1, j2):
        for t in range(3):
            copy_d(t, j1, j2, 1 - core).wait_recv()
        if hook is not None:
            hook(j1, j2)

    thirds = range(3)
    for t in thirds:
        start_a(t, 0, 0)
    for t in thirds:
        start_a(t, 1, 0)
    yield
    for d in range(2):
        for t in thirds:
            land_a(t, 0, 0, d)
            start_a(t, 1, 2 - d)
    yield
    for t in thirds:
        land_b(t, 0, 0)
        start_a(t, 1, 3)
    for t in thirds:
        start_a(t, 2, 0)
        copy_d(t, 0, 0, core).start()
    yield
    for j in range(4):
        for t in thirds:
            for d in range(2):
                land_a(t, 1, j, d)
        yield
    for j1 in (1, 2):
        for t in thirds:
            start_a(t, 2, j1)
            copy_d(t, j1, 0, core).start()
    for j in range(4):
        for t in thirds:
            land_b(t, 1, j)
    for t in thirds:
        start_a(t, 2, 3)
        copy_d(t, 3, 0, core).start()
    yield

    @pl.loop(0, 4)
    def _(j):
        for t in thirds:
            for d in range(2):
                land_a(t, 2, j, d)
                copy_d(t, j, 2 - d, core).start()
        line_done(j, 0)

    @pl.loop(0, 4)
    def _(j):
        for t in thirds:
            land_b(t, 2, j)
            copy_d(t, j, 3, core).start()
        line_done(j, 1)
        line_done(j, 2)

        @pl.when(j >= 1)
        def _():
            line_done(j - 1, 3)

    line_done(3, 3)

    for t in thirds:
        for p in range(3):
            for j in range(1 if p == 0 else 4):
                for d in range(2):
                    copy_a(t, p, j, d, 0).wait_send()
                    copy_b(t, p, j, d, 3 if d == 0 else 1).wait_send()

    @pl.loop(0, 4)
    def _(j1):
        @pl.loop(0, 4)
        def _(j2):
            for t in thirds:
                copy_d(t, j1, j2, core).wait_send()


def split(values, parts):
    out = []
    for _ in range(parts):
        out.append(values.astype(BF16))
        values = values - out[-1].astype(F32)
    return out


def dot(left, right, dims=((1,), (0,)), precision=None):
    return lax.dot_general(left, right, (dims, ((), ())), precision=precision, preferred_element_type=F32)


NT = ((1,), (1,))
TN = ((0,), (0,))


def factor_block(both, step):
    count, size, _ = both.shape
    block = 8
    shape = (count, block, size)
    sub = lax.broadcasted_iota(jnp.int32, shape, 1)
    lane = lax.broadcasted_iota(jnp.int32, shape, 2)
    base = pl.multiple_of(step * block, block)
    spread = lambda a, i: jnp.broadcast_to(a[:, i:i + 1, :], shape)
    band = both[:, pl.ds(base, block), :]
    upper, lower = band[:, :, :size], band[:, :, size:]
    turned = jnp.stack([pltpu.roll(upper[k], lax.rem(size - base, size), 1) for k in range(count)])
    columns = [jnp.broadcast_to(turned[:, :, i:i + 1], shape) for i in range(block)]
    inverse = jnp.zeros(shape, F32)
    for i in range(block):
        recip = 1.0 / spread(columns[i], i)
        factor = jnp.where(sub > i, columns[i] * recip, 0.0)
        inverse = jnp.where(sub == i, recip, inverse)
        for q in range(i + 1, block):
            columns[q] = columns[q] - factor * spread(columns[q], i)
        upper = upper - factor * spread(upper, i)
        lower = lower - factor * spread(lower, i)
    factors = jnp.where(lane >= base + block, upper * inverse, 0.0)
    rows = jnp.concatenate([upper, lower], 2)
    less = []
    for k in range(count):
        h, m, l = [p.astype(F32) for p in split(factors[k], 3)]
        first = jnp.concatenate([h, h, h, m, m, l], 0).astype(BF16)
        h, m, l = [p.astype(F32) for p in split(rows[k], 3)]
        less.append(dot(first, jnp.concatenate([h, m, l, h, m, h], 0).astype(BF16), TN))
    for k in range(count):
        both[k] = both[k] - less[k]
    both[:, pl.ds(base, block), :] = jnp.concatenate([upper, lower * jnp.sqrt(inverse)], 2)


def main_kernel(m_hbm, g_hbm, q_hbm, parts, qbuf, left_ref, scale_ref,
                mbuf, gbuf, part, zbuf, raw, stacked, both, full, other,
                ra0, rb0, ra1, rb1, ra2, rb2, pair, mix, squares, wide,
                q_sem, load_sem, z_send, z_recv, d_send, d_recv, s_send, s_recv, x_send, x_recv, *sems):
    place = Place()
    z, x, y = place.at
    core = place.core
    sems_q, sems_raw, sems_term = sems[:6], sems[6:12], sems[12:]
    count, stack_rows, width = parts.shape
    slots, _, rows, span = mbuf.shape
    chunks = width // span

    def columns(i):
        return pl.ds(pl.multiple_of(i * span, span), span)

    def load(i):
        slot = lax.rem(i, slots)
        return (pltpu.make_async_copy(m_hbm.at[:, :, columns(i)], mbuf.at[slot], load_sem.at[0, slot]),
                pltpu.make_async_copy(g_hbm.at[:, :, columns(i)], gbuf.at[slot], load_sem.at[1, slot]))

    def blend(first, last):
        @pl.loop(first, last)
        def _(i):
            slot = lax.rem(i, slots)
            for copy in load(i):
                copy.wait()
            for t in range(count):
                parts[t, :, columns(i)] = jnp.concatenate(split(mbuf[slot, t] + gbuf[slot, t], 3), 0)

            @pl.when(i + slots < chunks)
            def _():
                for copy in load(i + slots):
                    copy.start()

    loads = [pltpu.make_async_copy(q_hbm.at[:, pl.ds(t * RANK, RANK)], qbuf.at[t, z, x, y, core], q_sem.at[t])
             for t in range(3)]
    for copy in loads:
        copy.start()
    for i in range(slots):
        for copy in load(i):
            copy.start()
    greet(place, NEAR + [(0, 2)])
    for copy in loads:
        copy.wait()
    part[...] = jnp.zeros_like(part)

    def hook(j1, j2):
        @pl.loop(0, 3)
        def _(t):
            left, right = [], []
            for i in range(N):
                cz, cx, cy = place.line(t, j1, j2, i)
                column = pl.multiple_of(((cz * N + cx) * N + cy) * RANK, RANK)
                left.append(parts[t, :, pl.ds(column, RANK)])
                right.append(qbuf[t, cz, cx, cy].reshape(RANK, RANK))
            left = jnp.concatenate(left, 1)
            h, m, l = split(jnp.concatenate(right, 0), 3)
            out = dot(left, jnp.concatenate([h, m], 1))
            tile = lambda i, j: out[i * rows:(i + 1) * rows, j * RANK:(j + 1) * RANK]
            small = (tile(2, 0) + tile(1, 1)) + dot(left[:rows], l)
            part[t] += (small + (tile(1, 0) + tile(0, 1))) + tile(0, 0)

    done = 0
    for _ in gather(place, qbuf, sems_q, hook):
        if done < chunks:
            blend(done, min(done + 3, chunks))
            done += 3

    quarter = rows // N
    sends = []
    for d in (1, 2, 3):
        to = place.far(0, d)
        sends.append(pltpu.make_async_remote_copy(
            part.at[:, pl.ds(pl.multiple_of(to * quarter, quarter), quarter)], zbuf.at[d],
            z_send.at[d], z_recv.at[d], device_id=place.chip(0, d), device_id_type=MESH))
        sends[-1].start()
    zbuf[0] = part[:, pl.ds(pl.multiple_of(z * quarter, quarter), quarter)]
    for send in sends:
        send.wait_recv()
    total = ((zbuf[0] + zbuf[1]) + (zbuf[2] + zbuf[3])) * (1.0 / N)
    for t in range(3):
        raw[t, z, x, y, core] = total[t]
    for send in sends:
        send.wait_send()
    for _ in gather(place, raw, sems_raw):
        pass

    eye = (lax.broadcasted_iota(jnp.int32, (RANK, RANK), 0) == lax.broadcasted_iota(jnp.int32, (RANK, RANK), 1)).astype(F32)
    for t in range(3):
        h, m, l = [p.astype(F32) for p in split(raw[t, :, x, y, core].reshape(rows, RANK), 3)]
        none = jnp.zeros_like(h)
        pairs = [jnp.concatenate(pair, 1) for pair in ((h, l), (h, m), (h, none), (m, none))]
        stacked[t] = jnp.concatenate(pairs, 0).T.astype(BF16)

    def grams(inverse):
        if inverse:
            for t in range(3):
                h, m, l = split(mix[t].T, 3)
                wide[t] = jnp.concatenate([jnp.concatenate([h, m, l], 1), jnp.concatenate([m, h, h], 1)], 0)

        def add(i, grams):
            out = []
            for t in range(3):
                whole, low = grams[t]
                some = raw[t, i].reshape(512, RANK)
                h, m, l = split(some, 3)
                if inverse:
                    main = dot(jnp.concatenate([h, m], 1), wide[t, :, :2 * RANK])
                    rest = dot(jnp.concatenate([h, l], 1), wide[t, :, 2 * RANK:])
                    h, m, l = split(main[:, :RANK] + (main[:, RANK:] + rest), 3)
                all_ = dot(jnp.concatenate([h, m, l], 1), jnp.concatenate([h, m], 1), TN)
                tile = lambda i, j: all_[i * RANK:(i + 1) * RANK, j * RANK:(j + 1) * RANK]
                out.append((whole + (tile(0, 0) + ((tile(0, 1) + tile(1, 0)) + tile(1, 1))), low + tile(2, 0)))
            return tuple(out)

        zero = jnp.zeros((RANK, RANK), F32)
        for t, (whole, low) in enumerate(lax.fori_loop(0, N, add, ((zero, zero),) * 3)):
            both[t, :, :RANK] = whole + (low + low.T)
            both[t, :, RANK:] = eye

    grams(False)

    def swap(t, cz, cx):
        return pltpu.make_async_remote_copy(
            full.at[t, cz, cx, :, 1 - core], other.at[t, cz, cx], d_send.at[t, cz, cx], d_recv.at[t, cz, cx],
            device_id=place.sibling(), device_id_type=MESH)

    @pl.loop(0, N * N)
    def _(i):
        cz, cx = i // N, lax.rem(i, N)
        column = pl.multiple_of(i * (N * RANK), N * RANK)
        for t in range(3):
            right = parts[t, :, pl.ds(column, N * RANK)]
            out = dot(stacked[t], jnp.concatenate([right, right[:rows]], 0))
            out = out[:RANK] + out[RANK:]
            for cy in range(N):
                full[t, cz, cx, cy] = out[:, cy * RANK:(cy + 1) * RANK].reshape(2, RANK // 2, RANK)
        factor_block(both, i)
        for t in range(3):
            swap(t, cz, cx).start()

    for t in range(3):
        mix[t] = both[t, :, RANK:]
    grams(True)

    @pl.loop(0, N * N)
    def _(i):
        cz, cx = i // N, lax.rem(i, N)
        for t in range(3):
            swap(t, cz, cx).wait_recv()
            full[t, cz, cx, :, core] += other[t, cz, cx]

    half = RANK // 4
    first = (ra0, ra1, ra2)
    whole = (rb0, rb1, rb2)

    def index(t, q, da, part=None):
        where = [None] * 3
        for p in range(3):
            axis = axis_of(t, p)
            if p < 2 - q:
                where[axis] = slice(None)
            elif p == 2 - q:
                where[axis] = place.far(axis, da)
            else:
                where[axis] = place.at[axis]
        span = slice(None) if part is None else pl.ds(part * half, half)
        return (t, *where, core, span)

    def hop_a(t, q, d):
        return pltpu.make_async_remote_copy(
            full.at[index(t, q, 2, d)], first[q].at[t, d], s_send.at[t, q, 0, d], s_recv.at[t, q, 0, d],
            device_id=place.chip(axis_of(t, 2 - q), 1 if d == 0 else 3), device_id_type=MESH)

    def hop_b(t, q, d):
        return pltpu.make_async_remote_copy(
            full.at[index(t, q, 1 if d == 0 else 3)], whole[q].at[t, d], s_send.at[t, q, 1, d], s_recv.at[t, q, 1, d],
            device_id=place.chip(axis_of(t, 2 - q), 1 if d == 0 else 3), device_id_type=MESH)

    for q in range(3):
        for t in range(3):
            for d in range(2):
                hop_a(t, q, d).start()
        if q == 0:
            pl.loop(0, 8)(lambda i: factor_block(both, i))
        for t in range(3):
            for d in range(2):
                hop_a(t, q, d).wait_recv()
                spot = index(t, q, 1 if d == 0 else 3, d)
                full[spot] = full[spot] + first[q][t, d]
                hop_b(t, q, d).start()
        if q == 0:
            pl.loop(8, 16)(lambda i: factor_block(both, i))
            for t in range(3):
                left = dot(raw[t, :, x, y, core].reshape(rows, RANK), mix[t], NT, HIGH)
                inv = both[t, :, RANK:]
                left_ref[t] = dot(left, inv, NT, HIGH)
                mix[t] = dot(inv, mix[t], precision=HIGH) * (1.0 / N)
        for t in range(3):
            spot = index(t, q, 0)
            for d in range(2):
                hop_b(t, q, d).wait_recv()
                full[spot] = full[spot] + whole[q][t, d]

    for t in range(3):
        pair[t, core] = full[t, z, x, y, core]
    half_swap = pltpu.make_async_remote_copy(
        pair.at[:, core], pair.at[:, core], x_send, x_recv, device_id=place.sibling(), device_id_type=MESH)
    half_swap.start()
    pltpu.make_async_remote_copy(
        pair.at[:, 1 - core], pair.at[:, 1 - core], x_send, x_recv, device_id=place.sibling(),
        device_id_type=MESH).wait_recv()
    half_swap.wait_send()
    term = qbuf
    mine = pl.ds(pl.multiple_of(core * (RANK // 2), RANK // 2), RANK // 2)
    for t in range(3):
        term[t, z, x, y, core] = dot(mix[t, mine, :], pair[t].reshape(RANK, RANK), precision=HIGH)
    ones = jnp.ones((8, RANK), F32)

    def keep(j1, j2):
        for t in range(3):
            where = [slice(None)] * 3
            for p, j in ((1, j1), (2, j2)):
                where[axis_of(t, p)] = place.far(axis_of(t, p), dyn_off(j))
            block = term[(t, *where)].reshape(N, RANK, RANK)
            block = block * block
            total = (block[0] + block[1]) + (block[2] + block[3])
            squares[t, where[axis_of(t, 1)], where[axis_of(t, 2)]] = dot(ones, total, NT, HIGH)

    for _ in gather(place, term, sems_term, keep):
        pass
    for t in range(3):
        total = jnp.sum(squares[t].reshape(N * N, 8, RANK), axis=0)
        scale_ref[t] = 1.0 / jnp.sqrt(total + 1e-6)
    for q in range(3):
        for t in range(3):
            for d in range(2):
                hop_a(t, q, d).wait_send()
                hop_b(t, q, d).wait_send()

    @pl.loop(0, N)
    def _(cz):
        @pl.loop(0, N)
        def _(cx):
            for t in range(3):
                swap(t, cz, cx).wait_send()


def last_kernel(gain, parts_ref, term_ref, left_ref, scale_ref, next_ref, update_ref, basis_ref):
    t, i = pl.program_id(0), pl.program_id(1)
    rows, span = update_ref.shape[1:]
    scale = scale_ref[t, 0:1, :]
    left = left_ref[t]
    high, low = split(jnp.concatenate([left * 0.05, left * (scale * gain)], 0), 2)
    lhs = jnp.concatenate([jnp.concatenate([high, high], 1), jnp.concatenate([low, jnp.zeros_like(low)], 1)], 0)
    chips = span // RANK
    for j in range(chips // N):
        line = i * (chips // N) + j
        block = term_ref[t, line // N, lax.rem(line, N)].reshape(N, RANK, RANK)
        high, low = split(jnp.concatenate([block[c] for c in range(N)], 1), 2)
        out = dot(lhs, jnp.concatenate([high, low], 0))
        out = out[:2 * rows] + out[2 * rows:]
        here = slice(j * N * RANK, (j + 1) * N * RANK)
        column = pl.multiple_of(line * (N * RANK), N * RANK)
        h, m, l = [parts_ref[t, k * rows:(k + 1) * rows, pl.ds(column, N * RANK)].astype(F32) for k in range(3)]
        next_ref[0, 0, :, here] = (h + (m + l)) - out[:rows]
        update_ref[0, :, here] = out[rows:]

    @pl.when(i == 0)
    def _():
        place = Place()
        z, x, y = place.at
        basis = term_ref[t, z, x, y].reshape(RANK, RANK).T * scale
        basis_ref[...] = jnp.where(place.core == 0, basis[:64], basis[64:])


def body(momentum, gradient, basis):
    momentum, gradient = momentum[0], gradient[0]
    count, rows, width = momentum.shape
    chips = (N, N, N, 2)
    dma = pltpu.SemaphoreType.DMA
    f32 = lambda *shape: jax.ShapeDtypeStruct(shape, F32)
    room = lambda *shape: pltpu.VMEM(shape, F32)
    kept = [pltpu.VMEM((count, 3 * rows, width), BF16), room(3, *chips, 64, RANK)]
    parts, term, left, scale = pl.pallas_call(
        main_kernel,
        name="dion",
        out_shape=kept + [room(3, rows, RANK), room(3, 8, RANK)],
        in_specs=[ANY] * 3,
        out_specs=[VMEM] * 4,
        scratch_shapes=[
            room(4, count, rows, 512), room(4, count, rows, 512),
            room(count, rows, RANK), room(N, 3, 16, RANK), room(3, *chips, 16, RANK),
            pltpu.VMEM((3, 2 * RANK, 4 * rows), BF16), room(3, RANK, 2 * RANK),
            room(3, *chips, 64, RANK), room(3, N, N, N, 64, RANK),
            room(3, 2, N, N, 32, RANK), room(3, 2, N, N, 64, RANK),
            room(3, 2, N, 32, RANK), room(3, 2, N, 64, RANK),
            room(3, 2, 32, RANK), room(3, 2, 64, RANK),
            room(3, 2, 64, RANK), room(3, RANK, RANK), room(3, N, N, 8, RANK),
            pltpu.VMEM((3, 2 * RANK, 3 * RANK), BF16),
            dma((3,)), dma((2, 4)), dma((4,)), dma((4,)),
            dma((3, N, N)), dma((3, N, N)), dma((3, 3, 2, 2)), dma((3, 3, 2, 2)), dma, dma] + gather_sems() * 3,
        compiler_params=pltpu.CompilerParams(collective_id=0, has_side_effects=True, vmem_limit_bytes=40 * 2 ** 20),
    )(momentum, gradient, basis)
    gain = float((2048 * 8192 / RANK) ** 0.5)
    span = 2048
    parts, term, left, scale = [pltpu.with_memory_space_constraint(a, pltpu.VMEM) for a in (parts, term, left, scale)]
    return pl.pallas_call(
        functools.partial(last_kernel, gain),
        name="outputs",
        grid=(3, width // span),
        out_shape=[f32(1, count, rows, width), f32(count, rows, width), f32(64, 3 * RANK)],
        in_specs=[VMEM] * 4,
        out_specs=[
            pl.BlockSpec((1, 1, rows, span), lambda t, i: (0, t, 0, i)),
            pl.BlockSpec((1, rows, span), lambda t, i: (t, 0, i)),
            pl.BlockSpec((64, RANK), lambda t, i: (0, t)),
        ],
        compiler_params=pltpu.CompilerParams(vmem_limit_bytes=16 * 2 ** 20),
    )(parts, term, left, scale)


def solution(mesh):
    placed = (P("rep", None, "fsdp", None), P("rep", None, "fsdp", None), P(("rep", "fsdp"), None))
    return jax.shard_map(
        body,
        mesh=mesh,
        in_specs=placed,
        out_specs=(P("rep", None, "fsdp", None), P(None, "fsdp", None), P(("rep", "fsdp"), None)),
        check_vma=False,
    )
```

time: 940 us -> 180 us (0.19)
  waiting for transfers between devices: 610 us -> 0 us
  Pallas kernels: 0 us -> 179 us
  other arithmetic: 143 us -> 0 us
  matrix products: 64.8 us -> 0 us
  blocking collectives: 64.3 us -> 0 us
  local copies, waits for them, and re-layouts: 42.3 us -> 0 us
  between operations: 14.2 us -> 0.64 us
    psum x3 -> x0, waiting for transfers between devices: 240 us -> none  [the longest x2 201 us: body(): gram = lax.psum(gram, 'fsdp')]
    unnamed x7 -> x0, waiting for transfers between devices: 220 us -> none
    pallas_call x0 -> x2, Pallas kernels: none -> 179 us  [the longest x1 170 us: body(): pl.pallas_call(main_kernel, name='dion', out_shape=kept + [room(3, rows,...]
    all_gather x2 -> x0, waiting for transfers between devices: 150 us -> none  [the longest x1 80.2 us: body(): piece = lax.all_gather(basis, ('rep', 'fsdp'), axis=0, tiled=True)]
    another operation x12 -> x0, other arithmetic: 130 us -> none  [the longest x7 70.9 us: body(): lower = jnp.linalg.cholesky(gram)]
    psum x1 -> x0, blocking collectives: 64.3 us -> none  [body(): sums = lax.psum(jnp.sum(shard * shard, axis=0), ('rep', 'fsdp'))]
    dot_general x6 -> x0, matrix products: 63.3 us -> none  [the longest x1 18.5 us: body(): local = jnp.einsum('krc,cks->krs', columns, right, precision=HIGH)]
    all_gather x2 -> x0, local copies, waits for them, and re-layouts: 25.1 us -> none  [the longest x1 12.5 us: body(): piece = lax.all_gather(basis, ('rep', 'fsdp'), axis=0, tiled=True)]
  transfers between devices with their start and end apart: 6 -> 0, of which waited for: 6 -> 0; matrix products, arithmetic and copies ran while one was open for 0% -> 0% of each run, Pallas kernels for 0% -> 0%
where the time goes in v1:
time: 180 us
  Pallas kernels  179 us (99%)
    pallas_call x1, Pallas kernels, body(): pl.pallas_call(main_kernel, name='dion', out_shape=kept + [room(3, rows,...  170 us
    pallas_call x1, Pallas kernels, body(): pl.pallas_call(functools.partial(last_kernel, gain), name='outputs', grid...  9.35 us

profile of v1, /device:TPU:1, one launch (start us, length us, event | category | flops | bytes accessed | tf_op | source)
XLA Modules:
  0.0 179.7 jit_solution(11382593908760426697)
XLA Ops:
  0.6 169.7 %dion.1 = (bf16[3,192,8192]{2,1,0:T(8,128)(2,1)S(1)}, f32[3,4,4,4,2,64,128]{6,5,4,3,2,1,0:T(8,128)S(1)}, f32[3,64,128]{2,1,0:T(8,128)S(1)}, f32[3,8,128]{2,1,0:T(8,128)S(1)}) custom-call(f32[3,64,8192]{2,1,0:T(8,128)} %bitcast.2, f32[3,64,8192]{2,1,0:T(8,128)} %bitcast.3, f32[64,384]{1,0:T(8,128)} %q_hbm.1), custom_call_target="tpu_custom_call" | custom-call | tf_op jit(solution)/shard_map/dion/pallas_call | solution.py:544
  170.4 9.3 %outputs.1 = (f32[1,3,64,8192]{3,2,1,0:T(8,128)}, f32[3,64,8192]{2,1,0:T(8,128)}, f32[64,384]{1,0:T(8,128)}) custom-call(bf16[3,192,8192]{2,1,0:T(8,128)(2,1)S(1)} %get-tuple-element.7.parts_ref, f32[3,4,4,4,2,64,128]{6,5,4,3,2,1,0:T(8,128)S(1)} %get-tuple-element.8.term_ref, f32[3,64,128]{2,1,0:T(8,128)S(1)} %get-tuple-element.9.left_ref, ...), custom_call_target="tpu_custom_call" | custom-call | tf_op jit(solution)/shard_map/outputs/pallas_call | solution.py:567

commit v2 on v1

--- a/solution.py
+++ b/solution.py
@@ -74,7 +74,7 @@
     return [dma((3, 3, 4, 2))] * 4 + [dma((3, 4, 4))] * 2
 
 
-def gather(place, buf, sems, hook=None):
+def gather(place, buf, sems, hook=None, stepwise=False):
     send_a, recv_a, send_b, recv_b, send_d, recv_d = sems
     core = place.core
     rows = buf.shape[5]
@@ -170,26 +170,32 @@
         copy_d(t, 3, 0, core).start()
     yield
 
-    @pl.loop(0, 4)
-    def _(j):
+    def near(j):
         for t in thirds:
             for d in range(2):
                 land_a(t, 2, j, d)
                 copy_d(t, j, 2 - d, core).start()
         line_done(j, 0)
 
-    @pl.loop(0, 4)
-    def _(j):
+    def opposite(j):
         for t in thirds:
             land_b(t, 2, j)
             copy_d(t, j, 3, core).start()
         line_done(j, 1)
         line_done(j, 2)
-
-        @pl.when(j >= 1)
-        def _():
+        if not isinstance(j, int):
+            pl.when(j >= 1)(lambda: line_done(j - 1, 3))
+        elif j >= 1:
             line_done(j - 1, 3)
 
+    if stepwise:
+        for step in (near, opposite):
+            for j in range(4):
+                step(j)
+                yield
+    else:
+        pl.loop(0, 4)(near)
+        pl.loop(0, 4)(opposite)
     line_done(3, 3)
 
     for t in thirds:
@@ -225,40 +231,51 @@
 
 def factor_block(both, step):
     count, size, _ = both.shape
-    block = 8
-    shape = (count, block, size)
-    sub = lax.broadcasted_iota(jnp.int32, shape, 1)
-    lane = lax.broadcasted_iota(jnp.int32, shape, 2)
+    block, piece = 16, 8
+    lane = lax.broadcasted_iota(jnp.int32, (count, block, size), 2)
     base = pl.multiple_of(step * block, block)
-    spread = lambda a, i: jnp.broadcast_to(a[:, i:i + 1, :], shape)
     band = both[:, pl.ds(base, block), :]
     upper, lower = band[:, :, :size], band[:, :, size:]
-    turned = jnp.stack([pltpu.roll(upper[k], lax.rem(size - base, size), 1) for k in range(count)])
-    columns = [jnp.broadcast_to(turned[:, :, i:i + 1], shape) for i in range(block)]
-    inverse = jnp.zeros(shape, F32)
-    for i in range(block):
-        recip = 1.0 / spread(columns[i], i)
-        factor = jnp.where(sub > i, columns[i] * recip, 0.0)
-        inverse = jnp.where(sub == i, recip, inverse)
-        for q in range(i + 1, block):
-            columns[q] = columns[q] - factor * spread(columns[q], i)
-        upper = upper - factor * spread(upper, i)
-        lower = lower - factor * spread(lower, i)
+    inverses, done = [], []
+    for part in range(block // piece):
+        rows = block - part * piece
+        shape = (count, rows, size)
+        sub = lax.broadcasted_iota(jnp.int32, shape, 1)
+        spread = lambda a, i: jnp.broadcast_to(a[:, i:i + 1, :], shape)
+        turned = jnp.stack([pltpu.roll(upper[k], lax.rem(size - base, size), 1) for k in range(count)])
+        columns = [jnp.broadcast_to(turned[:, :, part * piece + i:part * piece + i + 1], shape) for i in range(piece)]
+        inverse = jnp.zeros((count, piece, size), F32)
+        for i in range(piece):
+            pivot = jnp.broadcast_to(columns[i][:, i:i + 1, :], (count, piece, size))
+            recip = pl.reciprocal(pivot, approx=True)
+            recip = recip * (2.0 - pivot * recip)
+            recip = recip * (2.0 - pivot * recip)
+            inverse = jnp.where(sub[:, :piece] == i, recip, inverse)
+            factor = jnp.where(sub > i, columns[i] * jnp.concatenate([recip] * (rows // piece), 1), 0.0)
+            for q in range(i + 1, piece):
+                columns[q] = columns[q] - factor * spread(columns[q], i)
+            upper = upper - factor * spread(upper, i)
+            lower = lower - factor * spread(lower, i)
+        inverses.append(inverse)
+        done.append((upper[:, :piece], lower[:, :piece]))
+        upper, lower = upper[:, piece:], lower[:, piece:]
+    upper, lower = [jnp.concatenate(half, 1) for half in zip(*done)]
+    inverse = jnp.concatenate(inverses, 1)
     factors = jnp.where(lane >= base + block, upper * inverse, 0.0)
     rows = jnp.concatenate([upper, lower], 2)
     less = []
     for k in range(count):
-        h, m, l = [p.astype(F32) for p in split(factors[k], 3)]
-        first = jnp.concatenate([h, h, h, m, m, l], 0).astype(BF16)
-        h, m, l = [p.astype(F32) for p in split(rows[k], 3)]
-        less.append(dot(first, jnp.concatenate([h, m, l, h, m, h], 0).astype(BF16), TN))
+        h, m, l = split(factors[k], 3)
+        first = jnp.concatenate([h, h, h, m, m, l], 0)
+        h, m, l = split(rows[k], 3)
+        less.append(dot(first, jnp.concatenate([h, m, l, h, m, h], 0), TN))
     for k in range(count):
         both[k] = both[k] - less[k]
     both[:, pl.ds(base, block), :] = jnp.concatenate([upper, lower * jnp.sqrt(inverse)], 2)
 
 
 def main_kernel(m_hbm, g_hbm, q_hbm, parts, qbuf, left_ref, scale_ref,
-                mbuf, gbuf, part, zbuf, raw, stacked, both, full, other,
+                mbuf, gbuf, part, zbuf, zown, raw, stacked, both, full, other,
                 ra0, rb0, ra1, rb1, ra2, rb2, pair, mix, squares, wide,
                 q_sem, load_sem, z_send, z_recv, d_send, d_recv, s_send, s_recv, x_send, x_recv, *sems):
     place = Place()
@@ -331,25 +348,155 @@
         to = place.far(0, d)
         sends.append(pltpu.make_async_remote_copy(
             part.at[:, pl.ds(pl.multiple_of(to * quarter, quarter), quarter)], zbuf.at[d],
-            z_send.at[d], z_recv.at[d], device_id=place.chip(0, d), device_id_type=MESH))
+            z_send.at[0, d], z_recv.at[0, d], device_id=place.chip(0, d), device_id_type=MESH))
         sends[-1].start()
     zbuf[0] = part[:, pl.ds(pl.multiple_of(z * quarter, quarter), quarter)]
     for send in sends:
         send.wait_recv()
     total = ((zbuf[0] + zbuf[1]) + (zbuf[2] + zbuf[3])) * (1.0 / N)
+    zown[z] = total
     for t in range(3):
         raw[t, z, x, y, core] = total[t]
-    for send in sends:
-        send.wait_send()
-    for _ in gather(place, raw, sems_raw):
-        pass
-
+    for d in (1, 2, 3):
+        sends.append(pltpu.make_async_remote_copy(
+            zown.at[z], zown.at[z], z_send.at[1, d], z_recv.at[1, d],
+            device_id=place.chip(0, d), device_id_type=MESH))
+        sends[-1].start()
+    rest = gather(place, raw, sems_raw, stepwise=True)
+    next(rest)
+    for d in (1, 2, 3):
+        spot = zown.at[place.far(0, N - d)]
+        pltpu.make_async_remote_copy(spot, spot, z_send.at[1, d], z_recv.at[1, d],
+                                     device_id=place.chip(0, d), device_id_type=MESH).wait_recv()
     eye = (lax.broadcasted_iota(jnp.int32, (RANK, RANK), 0) == lax.broadcasted_iota(jnp.int32, (RANK, RANK), 1)).astype(F32)
     for t in range(3):
-        h, m, l = [p.astype(F32) for p in split(raw[t, :, x, y, core].reshape(rows, RANK), 3)]
+        h, m, l = [p.astype(F32) for p in split(zown[:, t].reshape(rows, RANK), 3)]
         none = jnp.zeros_like(h)
         pairs = [jnp.concatenate(pair, 1) for pair in ((h, l), (h, m), (h, none), (m, none))]
         stacked[t] = jnp.concatenate(pairs, 0).T.astype(BF16)
+
+    half = RANK // 4
+
+    def spot(t, j1, j2, whose, part=None):
+        where = [slice(None)] * 3
+        for p, j in ((1, j1), (2, j2)):
+            where[axis_of(t, p)] = place.far(axis_of(t, p), OFF[j])
+        return (t, *where, whose, slice(None) if part is None else pl.ds(part * half, half))
+
+    def unit(t, j, part=None):
+        where = list(place.at)
+        where[axis_of(t, 0)] = place.far(axis_of(t, 0), OFF[j])
+        return (t, *where, core, slice(None) if part is None else pl.ds(part * half, half))
+
+    def swap(t, j1, j2):
+        return pltpu.make_async_remote_copy(
+            full.at[spot(t, j1, j2, 1 - core)], other.at[t, j1, j2], d_send.at[t, j1, j2], d_recv.at[t, j1, j2],
+            device_id=place.sibling(), device_id_type=MESH)
+
+    def hop(t, p, d, kind, j, src, dst):
+        return pltpu.make_async_remote_copy(
+            src, dst, s_send.at[t, p, kind, j, d], s_recv.at[t, p, kind, j, d],
+            device_id=place.chip(axis_of(t, p), 1 if d == 0 else 3), device_id_type=MESH)
+
+    def far_a(t, j, d):
+        return hop(t, 2, d, 0, j, full.at[spot(t, j, 3, core, d)], ra0.at[t, d, j])
+
+    def far_b(t, j, d):
+        return hop(t, 2, d, 1, j, full.at[spot(t, j, d + 1, core)], rb0.at[t, d, j])
+
+    def mid_a(t, d):
+        return hop(t, 1, d, 0, 0, full.at[spot(t, 3, 0, core, d)], ra1.at[t, d])
+
+    def mid_b(t, d):
+        return hop(t, 1, d, 1, 0, full.at[spot(t, d + 1, 0, core)], rb1.at[t, d])
+
+    def end_a(t, d):
+        return hop(t, 0, d, 0, 0, full.at[unit(t, 3, d)], ra2.at[t, d])
+
+    def end_b(t, d):
+        return hop(t, 0, d, 1, 0, full.at[unit(t, d + 1)], rb2.at[t, d])
+
+    def multiply(j1, j2):
+        @pl.loop(0, 3)
+        def _(t):
+            where = [place.line(t, j1, j2, i) for i in range(N)]
+            right = [parts[t, :, pl.ds(pl.multiple_of(((cz * N + cx) * N + cy) * RANK, RANK), RANK)] for cz, cx, cy in where]
+            right = jnp.concatenate(right, 1)
+            out = dot(stacked[t], jnp.concatenate([right, right[:rows]], 0))
+            out = out[:RANK] + out[RANK:]
+            for i, (cz, cx, cy) in enumerate(where):
+                full[t, cz, cx, cy] = out[:, i * RANK:(i + 1) * RANK].reshape(2, RANK // 2, RANK)
+        for t in range(3):
+            swap(t, j1, j2).start()
+
+    def settle(j1, j2):
+        for t in range(3):
+            swap(t, j1, j2).wait_recv()
+            here = spot(t, j1, j2, core)
+            full[here] = full[here] + other[t, j1, j2]
+            if j2 == 3:
+                for d in range(2):
+                    far_a(t, j1, d).start()
+            elif j2 > 0:
+                d = j2 - 1
+                far_a(t, j1, d).wait_recv()
+                here = spot(t, j1, j2, core, d)
+                full[here] = full[here] + ra0[t, d, j1]
+                far_b(t, j1, d).start()
+
+    lines = [(j1, j2) for j2 in (3, 2, 1, 0) for j1 in (3, 2, 1, 0)]
+    for i, line in enumerate(lines):
+        multiply(*line)
+        if i:
+            settle(*lines[i - 1])
+        next(rest, None)
+    settle(*lines[-1])
+    for _ in rest:
+        pass
+
+    def ring_ends():
+        for j in (3, 2, 1, 0):
+            for t in range(3):
+                here = spot(t, j, 0, core)
+                for d in range(2):
+                    far_b(t, j, d).wait_recv()
+                full[here] = full[here] + (rb0[t, 0, j] + rb0[t, 1, j])
+                if j == 3:
+                    for d in range(2):
+                        mid_a(t, d).start()
+        yield
+        for t in range(3):
+            for d in range(2):
+                mid_a(t, d).wait_recv()
+                here = spot(t, d + 1, 0, core, d)
+                full[here] = full[here] + ra1[t, d]
+                mid_b(t, d).start()
+        yield
+        for t in range(3):
+            here = spot(t, 0, 0, core)
+            for d in range(2):
+                mid_b(t, d).wait_recv()
+            full[here] = full[here] + (rb1[t, 0] + rb1[t, 1])
+            for d in range(2):
+                end_a(t, d).start()
+        yield
+        for t in range(3):
+            for d in range(2):
+                end_a(t, d).wait_recv()
+                here = unit(t, d + 1, d)
+                full[here] = full[here] + ra2[t, d]
+                end_b(t, d).start()
+        yield
+        for t in range(3):
+            here = unit(t, 0)
+            for d in range(2):
+                end_b(t, d).wait_recv()
+            pair[t, core] = full[here] + (rb2[t, 0] + rb2[t, 1])
+        half_swap.start()
+        yield
+
+    half_swap = pltpu.make_async_remote_copy(
+        pair.at[:, core], pair.at[:, core], x_send, x_recv, device_id=place.sibling(), device_id_type=MESH)
 
     def grams(inverse):
         if inverse:
@@ -378,94 +525,20 @@
             both[t, :, RANK:] = eye
 
     grams(False)
-
-    def swap(t, cz, cx):
-        return pltpu.make_async_remote_copy(
-            full.at[t, cz, cx, :, 1 - core], other.at[t, cz, cx], d_send.at[t, cz, cx], d_recv.at[t, cz, cx],
-            device_id=place.sibling(), device_id_type=MESH)
-
-    @pl.loop(0, N * N)
-    def _(i):
-        cz, cx = i // N, lax.rem(i, N)
-        column = pl.multiple_of(i * (N * RANK), N * RANK)
-        for t in range(3):
-            right = parts[t, :, pl.ds(column, N * RANK)]
-            out = dot(stacked[t], jnp.concatenate([right, right[:rows]], 0))
-            out = out[:RANK] + out[RANK:]
-            for cy in range(N):
-                full[t, cz, cx, cy] = out[:, cy * RANK:(cy + 1) * RANK].reshape(2, RANK // 2, RANK)
-        factor_block(both, i)
-        for t in range(3):
-            swap(t, cz, cx).start()
-
+    ends = ring_ends()
+    for i in range(0, 8, 2):
+        pl.loop(i, i + 2)(lambda i: factor_block(both, i))
+        next(ends)
     for t in range(3):
         mix[t] = both[t, :, RANK:]
     grams(True)
-
-    @pl.loop(0, N * N)
-    def _(i):
-        cz, cx = i // N, lax.rem(i, N)
-        for t in range(3):
-            swap(t, cz, cx).wait_recv()
-            full[t, cz, cx, :, core] += other[t, cz, cx]
-
-    half = RANK // 4
-    first = (ra0, ra1, ra2)
-    whole = (rb0, rb1, rb2)
-
-    def index(t, q, da, part=None):
-        where = [None] * 3
-        for p in range(3):
-            axis = axis_of(t, p)
-            if p < 2 - q:
-                where[axis] = slice(None)
-            elif p == 2 - q:
-                where[axis] = place.far(axis, da)
-            else:
-                where[axis] = place.at[axis]
-        span = slice(None) if part is None else pl.ds(part * half, half)
-        return (t, *where, core, span)
-
-    def hop_a(t, q, d):
-        return pltpu.make_async_remote_copy(
-            full.at[index(t, q, 2, d)], first[q].at[t, d], s_send.at[t, q, 0, d], s_recv.at[t, q, 0, d],
-            device_id=place.chip(axis_of(t, 2 - q), 1 if d == 0 else 3), device_id_type=MESH)
-
-    def hop_b(t, q, d):
-        return pltpu.make_async_remote_copy(
-            full.at[index(t, q, 1 if d == 0 else 3)], whole[q].at[t, d], s_send.at[t, q, 1, d], s_recv.at[t, q, 1, d],
-            device_id=place.chip(axis_of(t, 2 - q), 1 if d == 0 else 3), device_id_type=MESH)
-
-    for q in range(3):
-        for t in range(3):
-            for d in range(2):
-                hop_a(t, q, d).start()
-        if q == 0:
-            pl.loop(0, 8)(lambda i: factor_block(both, i))
-        for t in range(3):
-            for d in range(2):
-                hop_a(t, q, d).wait_recv()
-                spot = index(t, q, 1 if d == 0 else 3, d)
-                full[spot] = full[spot] + first[q][t, d]
-                hop_b(t, q, d).start()
-        if q == 0:
-            pl.loop(8, 16)(lambda i: factor_block(both, i))
-            for t in range(3):
-                left = dot(raw[t, :, x, y, core].reshape(rows, RANK), mix[t], NT, HIGH)
-                inv = both[t, :, RANK:]
-                left_ref[t] = dot(left, inv, NT, HIGH)
-                mix[t] = dot(inv, mix[t], precision=HIGH) * (1.0 / N)
-        for t in range(3):
-            spot = index(t, q, 0)
-            for d in range(2):
-                hop_b(t, q, d).wait_recv()
-                full[spot] = full[spot] + whole[q][t, d]
-
+    next(ends)
+    pl.loop(0, 8)(lambda i: factor_block(both, i))
     for t in range(3):
-        pair[t, core] = full[t, z, x, y, core]
-    half_swap = pltpu.make_async_remote_copy(
-        pair.at[:, core], pair.at[:, core], x_send, x_recv, device_id=place.sibling(), device_id_type=MESH)
-    half_swap.start()
+        left = dot(zown[:, t].reshape(rows, RANK), mix[t], NT, HIGH)
+        inv = both[t, :, RANK:]
+        left_ref[t] = dot(left, inv, NT, HIGH)
+        mix[t] = dot(inv, mix[t], precision=HIGH) * (1.0 / N)
     pltpu.make_async_remote_copy(
         pair.at[:, 1 - core], pair.at[:, 1 - core], x_send, x_recv, device_id=place.sibling(),
         device_id_type=MESH).wait_recv()
@@ -491,18 +564,17 @@
     for t in range(3):
         total = jnp.sum(squares[t].reshape(N * N, 8, RANK), axis=0)
         scale_ref[t] = 1.0 / jnp.sqrt(total + 1e-6)
-    for q in range(3):
-        for t in range(3):
-            for d in range(2):
-                hop_a(t, q, d).wait_send()
-                hop_b(t, q, d).wait_send()
-
-    @pl.loop(0, N)
-    def _(cz):
-        @pl.loop(0, N)
-        def _(cx):
-            for t in range(3):
-                swap(t, cz, cx).wait_send()
+    for send in sends:
+        send.wait_send()
+    for t in range(3):
+        for d in range(2):
+            for j in range(N):
+                far_a(t, j, d).wait_send()
+                far_b(t, j, d).wait_send()
+            for copy in (mid_a, mid_b, end_a, end_b):
+                copy(t, d).wait_send()
+        for j1, j2 in lines:
+            swap(t, j1, j2).wait_send()
 
 
 def last_kernel(gain, parts_ref, term_ref, left_ref, scale_ref, next_ref, update_ref, basis_ref):
@@ -549,7 +621,7 @@
         out_specs=[VMEM] * 4,
         scratch_shapes=[
             room(4, count, rows, 512), room(4, count, rows, 512),
-            room(count, rows, RANK), room(N, 3, 16, RANK), room(3, *chips, 16, RANK),
+            room(count, rows, RANK), room(N, 3, 16, RANK), room(N, 3, 16, RANK), room(3, *chips, 16, RANK),
             pltpu.VMEM((3, 2 * RANK, 4 * rows), BF16), room(3, RANK, 2 * RANK),
             room(3, *chips, 64, RANK), room(3, N, N, N, 64, RANK),
             room(3, 2, N, N, 32, RANK), room(3, 2, N, N, 64, RANK),
@@ -557,8 +629,8 @@
             room(3, 2, 32, RANK), room(3, 2, 64, RANK),
             room(3, 2, 64, RANK), room(3, RANK, RANK), room(3, N, N, 8, RANK),
             pltpu.VMEM((3, 2 * RANK, 3 * RANK), BF16),
-            dma((3,)), dma((2, 4)), dma((4,)), dma((4,)),
-            dma((3, N, N)), dma((3, N, N)), dma((3, 3, 2, 2)), dma((3, 3, 2, 2)), dma, dma] + gather_sems() * 3,
+            dma((3,)), dma((2, 4)), dma((2, 4)), dma((2, 4)),
+            dma((3, N, N)), dma((3, N, N)), dma((3, 3, 2, N, 2)), dma((3, 3, 2, N, 2)), dma, dma] + gather_sems() * 3,
         compiler_params=pltpu.CompilerParams(collective_id=0, has_side_effects=True, vmem_limit_bytes=40 * 2 ** 20),
     )(momentum, gradient, basis)
     gain = float((2048 * 8192 / RANK) ** 0.5)

time: 180 us -> 170 us (0.944)
  Pallas kernels: 179 us -> 169 us
    pallas_call x1, Pallas kernels: 170 us -> 160 us  [body(): pl.pallas_call(main_kernel, name='dion', out_shape=kept + [room(3, rows,...]
where the time goes in v2:
time: 170 us
  Pallas kernels  169 us (99%)
    pallas_call x1, Pallas kernels, body(): pl.pallas_call(main_kernel, name='dion', out_shape=kept + [room(3, rows,...  160 us
    pallas_call x1, Pallas kernels, body(): pl.pallas_call(functools.partial(last_kernel, gain), name='outputs', grid...  9.34 us

profile of v2, /device:TPU:1, one launch (start us, length us, event | category | flops | bytes accessed | tf_op | source)
XLA Modules:
  0.0 169.9 jit_solution(13215919086138521596)
XLA Ops:
  0.6 159.9 %dion.1 = (bf16[3,192,8192]{2,1,0:T(8,128)(2,1)S(1)}, f32[3,4,4,4,2,64,128]{6,5,4,3,2,1,0:T(8,128)S(1)}, f32[3,64,128]{2,1,0:T(8,128)S(1)}, f32[3,8,128]{2,1,0:T(8,128)S(1)}) custom-call(f32[3,64,8192]{2,1,0:T(8,128)} %bitcast.2, f32[3,64,8192]{2,1,0:T(8,128)} %bitcast.3, f32[64,384]{1,0:T(8,128)} %q_hbm.1), custom_call_target="tpu_custom_call" | custom-call | tf_op jit(solution)/shard_map/dion/pallas_call | solution.py:616
  160.6 9.3 %outputs.1 = (f32[1,3,64,8192]{3,2,1,0:T(8,128)}, f32[3,64,8192]{2,1,0:T(8,128)}, f32[64,384]{1,0:T(8,128)}) custom-call(bf16[3,192,8192]{2,1,0:T(8,128)(2,1)S(1)} %get-tuple-element.7.parts_ref, f32[3,4,4,4,2,64,128]{6,5,4,3,2,1,0:T(8,128)S(1)} %get-tuple-element.8.term_ref, f32[3,64,128]{2,1,0:T(8,128)S(1)} %get-tuple-element.9.left_ref, ...), custom_call_target="tpu_custom_call" | custom-call | tf_op jit(solution)/shard_map/outputs/pallas_call | solution.py:639

commit v3 on v2

--- a/solution.py
+++ b/solution.py
@@ -274,10 +274,10 @@
     both[:, pl.ds(base, block), :] = jnp.concatenate([upper, lower * jnp.sqrt(inverse)], 2)
 
 
-def main_kernel(m_hbm, g_hbm, q_hbm, parts, qbuf, left_ref, scale_ref,
-                mbuf, gbuf, part, zbuf, zown, raw, stacked, both, full, other,
-                ra0, rb0, ra1, rb1, ra2, rb2, pair, mix, squares, wide,
-                q_sem, load_sem, z_send, z_recv, d_send, d_recv, s_send, s_recv, x_send, x_recv, *sems):
+def main_kernel(gain, m_hbm, g_hbm, q_hbm, full, basis_ref, parts, qbuf, left_ref, lhs, norms,
+                mbuf, gbuf, part, zbuf, zown, raw, stacked, both, other,
+                ra0, rb0, ra1, rb1, ra2, rb2, pair, mix, wide,
+                q_sem, load_sem, z_send, z_recv, d_send, d_recv, s_send, s_recv, x_send, x_recv, n_send, n_recv, *sems):
     place = Place()
     z, x, y = place.at
     core = place.core
@@ -315,7 +315,7 @@
     for i in range(slots):
         for copy in load(i):
             copy.start()
-    greet(place, NEAR + [(0, 2)])
+    greet(place, NEAR + [(0, 2), (1, 2), (2, 2)])
     for copy in loads:
         copy.wait()
     part[...] = jnp.zeros_like(part)
@@ -509,12 +509,12 @@
             for t in range(3):
                 whole, low = grams[t]
                 some = raw[t, i].reshape(512, RANK)
-                h, m, l = split(some, 3)
                 if inverse:
+                    h, m, l = split(some, 3)
                     main = dot(jnp.concatenate([h, m], 1), wide[t, :, :2 * RANK])
                     rest = dot(jnp.concatenate([h, l], 1), wide[t, :, 2 * RANK:])
-                    h, m, l = split(main[:, :RANK] + (main[:, RANK:] + rest), 3)
-                all_ = dot(jnp.concatenate([h, m, l], 1), jnp.concatenate([h, m], 1), TN)
+                    some = main[:, :RANK] + (main[:, RANK:] + rest)
+                all_ = dot(jnp.concatenate(split(some.T, 3), 0), jnp.concatenate(split(some, 2), 1))
                 tile = lambda i, j: all_[i * RANK:(i + 1) * RANK, j * RANK:(j + 1) * RANK]
                 out.append((whole + (tile(0, 0) + ((tile(0, 1) + tile(1, 0)) + tile(1, 1))), low + tile(2, 0)))
             return tuple(out)
@@ -543,27 +543,6 @@
         pair.at[:, 1 - core], pair.at[:, 1 - core], x_send, x_recv, device_id=place.sibling(),
         device_id_type=MESH).wait_recv()
     half_swap.wait_send()
-    term = qbuf
-    mine = pl.ds(pl.multiple_of(core * (RANK // 2), RANK // 2), RANK // 2)
-    for t in range(3):
-        term[t, z, x, y, core] = dot(mix[t, mine, :], pair[t].reshape(RANK, RANK), precision=HIGH)
-    ones = jnp.ones((8, RANK), F32)
-
-    def keep(j1, j2):
-        for t in range(3):
-            where = [slice(None)] * 3
-            for p, j in ((1, j1), (2, j2)):
-                where[axis_of(t, p)] = place.far(axis_of(t, p), dyn_off(j))
-            block = term[(t, *where)].reshape(N, RANK, RANK)
-            block = block * block
-            total = (block[0] + block[1]) + (block[2] + block[3])
-            squares[t, where[axis_of(t, 1)], where[axis_of(t, 2)]] = dot(ones, total, NT, HIGH)
-
-    for _ in gather(place, term, sems_term, keep):
-        pass
-    for t in range(3):
-        total = jnp.sum(squares[t].reshape(N * N, 8, RANK), axis=0)
-        scale_ref[t] = 1.0 / jnp.sqrt(total + 1e-6)
     for send in sends:
         send.wait_send()
     for t in range(3):
@@ -576,33 +555,79 @@
         for j1, j2 in lines:
             swap(t, j1, j2).wait_send()
 
-
-def last_kernel(gain, parts_ref, term_ref, left_ref, scale_ref, next_ref, update_ref, basis_ref):
+    term = qbuf
+    mine = pl.ds(pl.multiple_of(core * (RANK // 2), RANK // 2), RANK // 2)
+    ones = jnp.ones((8, RANK), F32)
+    own = lax.broadcasted_iota(jnp.int32, (RANK, RANK), 0) // (RANK // 2) == core
+    for t in range(3):
+        whole = dot(mix[t], pair[t].reshape(RANK, RANK), precision=HIGH)
+        pair[t] = whole.reshape(2, RANK // 2, RANK)
+        term[t, z, x, y, core] = pair[t, core]
+        norms[0, core, t] = dot(ones, jnp.where(own, whole * whole, 0.0), NT, HIGH)
+
+    def tell(stage, where, peer, sem):
+        return pltpu.make_async_remote_copy(norms.at[stage, where], norms.at[stage, where], n_send.at[stage, sem],
+                                            n_recv.at[stage, sem], device_id=peer, device_id_type=MESH)
+
+    def sum_norms():
+        tell(0, core, place.sibling(), 0).start()
+        yield
+        tell(0, 1 - core, place.sibling(), 0).wait_recv()
+        total = norms[0, 0] + norms[0, 1]
+        for axis in range(3):
+            stage = 1 + axis
+            here = place.at[axis]
+            norms[stage, here] = total
+            for d in (1, 2, 3):
+                tell(stage, here, place.chip(axis, d), d).start()
+            yield
+            for d in (1, 2, 3):
+                tell(stage, place.far(axis, N - d), place.chip(axis, d), d).wait_recv()
+            total = (norms[stage, 0] + norms[stage, 1]) + (norms[stage, 2] + norms[stage, 3])
+        scales = 1.0 / jnp.sqrt(total + 1e-6)
+        for t in range(3):
+            scale = scales[t, 0:1]
+            left = left_ref[t]
+            high, low = split(jnp.concatenate([left * 0.05, left * (scale * gain)], 0), 2)
+            lhs[t] = jnp.concatenate(
+                [jnp.concatenate([high, high], 1), jnp.concatenate([low, jnp.zeros_like(low)], 1)], 0)
+            basis = pair[t].reshape(RANK, RANK).T * scale
+            basis_ref[:, t * RANK:(t + 1) * RANK] = jnp.where(core == 0, basis[:RANK // 2], basis[RANK // 2:])
+        tell(0, core, place.sibling(), 0).wait_send()
+        for axis in range(3):
+            for d in (1, 2, 3):
+                tell(1 + axis, place.at[axis], place.chip(axis, d), d).wait_send()
+        yield
+
+    def emit(j1, j2):
+        @pl.loop(0, 3)
+        def _(t):
+            where = [place.line(t, j1, j2, i) for i in range(N)]
+            block = jnp.concatenate([term[t, cz, cx, cy].reshape(RANK, RANK) for cz, cx, cy in where], 1)
+            out = dot(lhs[t], jnp.concatenate(split(block, 2), 0))
+            out = out[:RANK] + out[RANK:]
+            for i, (cz, cx, cy) in enumerate(where):
+                column = pl.ds(pl.multiple_of(((cz * N + cx) * N + cy) * RANK, RANK), RANK)
+                tile = slice(i * RANK, (i + 1) * RANK)
+                h, m, l = [parts[t, k * rows:(k + 1) * rows, column].astype(F32) for k in range(3)]
+                full[t, cz, cx, cy, 0] = (h + (m + l)) - out[:rows, tile]
+                full[t, cz, cx, cy, 1] = out[rows:, tile]
+
+    norm_steps = sum_norms()
+    next(norm_steps)
+    for _ in gather(place, term, sems_term, emit):
+        next(norm_steps, None)
+
+
+def last_kernel(both_ref, basis_in, next_ref, update_ref, basis_ref):
     t, i = pl.program_id(0), pl.program_id(1)
-    rows, span = update_ref.shape[1:]
-    scale = scale_ref[t, 0:1, :]
-    left = left_ref[t]
-    high, low = split(jnp.concatenate([left * 0.05, left * (scale * gain)], 0), 2)
-    lhs = jnp.concatenate([jnp.concatenate([high, high], 1), jnp.concatenate([low, jnp.zeros_like(low)], 1)], 0)
-    chips = span // RANK
-    for j in range(chips // N):
-        line = i * (chips // N) + j
-        block = term_ref[t, line // N, lax.rem(line, N)].reshape(N, RANK, RANK)
-        high, low = split(jnp.concatenate([block[c] for c in range(N)], 1), 2)
-        out = dot(lhs, jnp.concatenate([high, low], 0))
-        out = out[:2 * rows] + out[2 * rows:]
-        here = slice(j * N * RANK, (j + 1) * N * RANK)
-        column = pl.multiple_of(line * (N * RANK), N * RANK)
-        h, m, l = [parts_ref[t, k * rows:(k + 1) * rows, pl.ds(column, N * RANK)].astype(F32) for k in range(3)]
-        next_ref[0, 0, :, here] = (h + (m + l)) - out[:rows]
-        update_ref[0, :, here] = out[rows:]
-
-    @pl.when(i == 0)
-    def _():
-        place = Place()
-        z, x, y = place.at
-        basis = term_ref[t, z, x, y].reshape(RANK, RANK).T * scale
-        basis_ref[...] = jnp.where(place.core == 0, basis[:64], basis[64:])
+    count = update_ref.shape[2] // RANK
+    for j in range(count):
+        chip = i * count + j
+        where = (t, chip // (N * N), lax.rem(chip // N, N), lax.rem(chip, N))
+        next_ref[0, 0, :, j * RANK:(j + 1) * RANK] = both_ref[(*where, 0)]
+        update_ref[0, :, j * RANK:(j + 1) * RANK] = both_ref[(*where, 1)]
+    basis_ref[...] = basis_in[...]
 
 
 def body(momentum, gradient, basis):
@@ -612,43 +637,44 @@
     dma = pltpu.SemaphoreType.DMA
     f32 = lambda *shape: jax.ShapeDtypeStruct(shape, F32)
     room = lambda *shape: pltpu.VMEM(shape, F32)
-    kept = [pltpu.VMEM((count, 3 * rows, width), BF16), room(3, *chips, 64, RANK)]
-    parts, term, left, scale = pl.pallas_call(
-        main_kernel,
+    gain = float((2048 * 8192 / RANK) ** 0.5)
+    full, basis_next = pl.pallas_call(
+        functools.partial(main_kernel, gain),
         name="dion",
-        out_shape=kept + [room(3, rows, RANK), room(3, 8, RANK)],
+        out_shape=[room(3, *chips, 64, RANK), room(64, 3 * RANK)],
         in_specs=[ANY] * 3,
-        out_specs=[VMEM] * 4,
+        out_specs=[VMEM] * 2,
         scratch_shapes=[
+            pltpu.VMEM((count, 3 * rows, width), BF16), room(3, *chips, 64, RANK), room(3, rows, RANK),
+            pltpu.VMEM((3, 2 * RANK, 2 * RANK), BF16), room(4, N, 3, 8, RANK),
             room(4, count, rows, 512), room(4, count, rows, 512),
             room(count, rows, RANK), room(N, 3, 16, RANK), room(N, 3, 16, RANK), room(3, *chips, 16, RANK),
             pltpu.VMEM((3, 2 * RANK, 4 * rows), BF16), room(3, RANK, 2 * RANK),
-            room(3, *chips, 64, RANK), room(3, N, N, N, 64, RANK),
+            room(3, N, N, N, 64, RANK),
             room(3, 2, N, N, 32, RANK), room(3, 2, N, N, 64, RANK),
             room(3, 2, N, 32, RANK), room(3, 2, N, 64, RANK),
             room(3, 2, 32, RANK), room(3, 2, 64, RANK),
-            room(3, 2, 64, RANK), room(3, RANK, RANK), room(3, N, N, 8, RANK),
+            room(3, 2, 64, RANK), room(3, RANK, RANK),
             pltpu.VMEM((3, 2 * RANK, 3 * RANK), BF16),
             dma((3,)), dma((2, 4)), dma((2, 4)), dma((2, 4)),
-            dma((3, N, N)), dma((3, N, N)), dma((3, 3, 2, N, 2)), dma((3, 3, 2, N, 2)), dma, dma] + gather_sems() * 3,
-        compiler_params=pltpu.CompilerParams(collective_id=0, has_side_effects=True, vmem_limit_bytes=40 * 2 ** 20),
+            dma((3, N, N)), dma((3, N, N)), dma((3, 3, 2, N, 2)), dma((3, 3, 2, N, 2)), dma, dma, dma((4, 4)), dma((4, 4))] + gather_sems() * 3,
+        compiler_params=pltpu.CompilerParams(collective_id=0, has_side_effects=True, vmem_limit_bytes=49 * 2 ** 20),
     )(momentum, gradient, basis)
-    gain = float((2048 * 8192 / RANK) ** 0.5)
     span = 2048
-    parts, term, left, scale = [pltpu.with_memory_space_constraint(a, pltpu.VMEM) for a in (parts, term, left, scale)]
+    full, basis_next = [pltpu.with_memory_space_constraint(a, pltpu.VMEM) for a in (full, basis_next)]
     return pl.pallas_call(
-        functools.partial(last_kernel, gain),
+        last_kernel,
         name="outputs",
         grid=(3, width // span),
         out_shape=[f32(1, count, rows, width), f32(count, rows, width), f32(64, 3 * RANK)],
-        in_specs=[VMEM] * 4,
+        in_specs=[VMEM] * 2,
         out_specs=[
             pl.BlockSpec((1, 1, rows, span), lambda t, i: (0, t, 0, i)),
             pl.BlockSpec((1, rows, span), lambda t, i: (t, 0, i)),
-            pl.BlockSpec((64, RANK), lambda t, i: (0, t)),
+            pl.BlockSpec((64, 3 * RANK), lambda t, i: (0, 0)),
         ],
         compiler_params=pltpu.CompilerParams(vmem_limit_bytes=16 * 2 ** 20),
-    )(parts, term, left, scale)
+    )(full, basis_next)
 
 
 def solution(mesh):

time: 170 us -> 173 us (1.018)
  Pallas kernels: 169 us -> 173 us
    pallas_call x2, Pallas kernels: 169 us -> 173 us  [the longest x1 166 us: body(): pl.pallas_call(functools.partial(main_kernel, gain), name='dion', out_sha...]
where the time goes in v3:
time: 173 us
  Pallas kernels  173 us (100%)
    pallas_call x1, Pallas kernels, body(): pl.pallas_call(functools.partial(main_kernel, gain), name='dion', out_sha...  166 us
    pallas_call x1, Pallas kernels, body(): pl.pallas_call(last_kernel, name='outputs', grid=(3, width // span), out_...  7.07 us

profile of v3, /device:TPU:1, one launch (start us, length us, event | category | flops | bytes accessed | tf_op | source)
XLA Modules:
  0.0 173.2 jit_solution(876746222741924537)
XLA Ops:
  0.6 165.5 %dion.1 = (f32[3,4,4,4,2,64,128]{6,5,4,3,2,1,0:T(8,128)S(1)}, f32[64,384]{1,0:T(8,128)S(1)}) custom-call(f32[3,64,8192]{2,1,0:T(8,128)} %bitcast.2, f32[3,64,8192]{2,1,0:T(8,128)} %bitcast.3, f32[64,384]{1,0:T(8,128)} %q_hbm.1), custom_call_target="tpu_custom_call" | custom-call | tf_op jit(solution)/shard_map/dion/pallas_call | solution.py:641
  166.2 7.1 %outputs.1 = (f32[1,3,64,8192]{3,2,1,0:T(8,128)}, f32[3,64,8192]{2,1,0:T(8,128)}, f32[64,384]{1,0:T(8,128)}) custom-call(f32[3,4,4,4,2,64,128]{6,5,4,3,2,1,0:T(8,128)S(1)} %get-tuple-element.5.both_ref, f32[64,384]{1,0:T(8,128)S(1)} %get-tuple-element.6.basis_in), custom_call_target="tpu_custom_call" | custom-call | tf_op jit(solution)/shard_map/outputs/pallas_call | solution.py:665

commit v4 on v3

--- a/solution.py
+++ b/solution.py
@@ -13,7 +13,6 @@
 BF16 = jnp.bfloat16
 RANK = 128
 N = 4
-OFF = (0, 1, 3, 2)
 ANY = pl.BlockSpec(memory_space=pl.ANY)
 VMEM = pl.BlockSpec(memory_space=pltpu.VMEM)
 
@@ -42,14 +41,23 @@
     def sibling(self):
         return (self.rep, self.fsdp + 1 - 2 * self.core)
 
-    def line(self, third, j1, j2, i):
-        off1, off2 = dyn_off(j1), dyn_off(j2)
+    def chips(self, t, j1, j2):
+        where = [None] * 3
+        where[axis_of(t, 1)] = self.far(axis_of(t, 1), dyn_off(j1))
+        where[axis_of(t, 2)] = self.far(axis_of(t, 2), dyn_off(j2))
+        out = []
+        for i in range(N):
+            where[axis_of(t, 0)] = i
+            out.append(tuple(where))
+        return out
+
+    def line(self, third, middle, distance, i):
         places = []
         for t in range(3):
             where = [None] * 3
             where[axis_of(t, 0)] = i
-            where[axis_of(t, 1)] = self.far(axis_of(t, 1), off1)
-            where[axis_of(t, 2)] = self.far(axis_of(t, 2), off2)
+            where[axis_of(t, 1)] = middle
+            where[axis_of(t, 2)] = self.far(axis_of(t, 2), distance)
             places.append(where)
         return [jnp.where(third == 0, a, jnp.where(third == 1, b, c)) for a, b, c in zip(*places)]
 
@@ -66,15 +74,114 @@
     pl.semaphore_wait(barrier, len(peers))
 
 
+OFF = (0, 1, 3, 2)
 NEAR = [(axis, d) for axis in range(3) for d in (1, 3)]
+
+
+def await_landed(place, spot, sem):
+    pltpu.make_async_remote_copy(spot, spot, sem, sem, device_id=place.sibling(), device_id_type=MESH).wait_recv()
+
+
+def await_sent(place, spot, sem):
+    pltpu.make_async_remote_copy(spot, spot, sem, sem, device_id=place.sibling(), device_id_type=MESH).wait_send()
 
 
 def gather_sems():
     dma = pltpu.SemaphoreType.DMA
+    return [dma((3,)), dma((3, 4)), dma((3, 2)), dma, dma((7,))]
+
+
+def gather(place, buf, sems, hook=None):
+    sent, recv_a, recv_b, sent_d, recv_d = sems
+    core = place.core
+    half = buf.shape[5] // 2
+    thirds = range(3)
+
+    def spot(t, p, distance, whose, part=None, middle=slice(None)):
+        where = [None] * 3
+        for q in range(3):
+            axis = axis_of(t, q)
+            if q < p:
+                where[axis] = middle if q == 1 else slice(None)
+            elif q == p:
+                where[axis] = place.far(axis, distance)
+            else:
+                where[axis] = place.at[axis]
+        return buf.at[(t, *where, whose, slice(None) if part is None else pl.ds(part * half, half))]
+
+    def send(t, p, d, block, sem):
+        pltpu.make_async_remote_copy(
+            block, block, sent.at[p], sem,
+            device_id=place.chip(axis_of(t, p), 1 if d == 0 else 3), device_id_type=MESH).start()
+
+    def share(block, n):
+        pltpu.make_async_remote_copy(
+            block, block, sent_d, recv_d.at[n], device_id=place.sibling(), device_id_type=MESH).start()
+
+    def size(p, whose, pieces=N):
+        if p == 0:
+            return buf.at[:, 0, 0, 0, whose]
+        if p == 1:
+            return buf.at[:, 0, 0, :, whose]
+        return buf.at[:, 0, pl.ds(0, pieces), :, whose]
+
+    came = (3, 1)
+    for p in (0, 1):
+        for t in thirds:
+            for d in range(2):
+                send(t, p, d, spot(t, p, 0, core), recv_a.at[p, d])
+        yield
+        for d in range(2):
+            await_landed(place, size(p, core), recv_a.at[p, d])
+            for t in thirds:
+                send(t, p, d, spot(t, p, came[d], core, d), recv_b.at[p, 0])
+        yield
+        await_landed(place, size(p, core), recv_b.at[p, 0])
+    run = hook if hook is not None else lambda *_: None
+    piece = lambda c: pl.ds(2 * c, 2)
+    for c in range(2):
+        for t in thirds:
+            for d in range(2):
+                send(t, 2, d, spot(t, 2, 0, core, None, piece(c)), recv_a.at[2, 2 * c + d])
+    for t in thirds:
+        share(spot(t, 2, 0, core), 0)
+    yield
+    await_landed(place, size(2, 1 - core), recv_d.at[0])
+    run(0, 0, N)
+    for c in range(2):
+        for d in range(2):
+            await_landed(place, size(2, core, 2), recv_a.at[2, 2 * c + d])
+            for t in thirds:
+                send(t, 2, d, spot(t, 2, came[d], core, d, piece(c)), recv_b.at[2, c])
+        for d in range(2):
+            for t in thirds:
+                share(spot(t, 2, came[d], core, None, piece(c)), 1 + 2 * c + d)
+        yield
+        if c == 0:
+            for d in range(2):
+                await_landed(place, size(2, 1 - core, 2), recv_d.at[1 + d])
+                run(came[d], 0, 2)
+    for c in range(2):
+        await_landed(place, size(2, core, 2), recv_b.at[2, c])
+        for t in thirds:
+            share(spot(t, 2, 2, core, None, piece(c)), 5 + c)
+        await_landed(place, size(2, 1 - core, 2), recv_d.at[3 + c])
+        run(came[c], 2, 2)
+    for c in range(2):
+        await_landed(place, size(2, 1 - core, 2), recv_d.at[5 + c])
+        run(2, 2 * c, 2)
+    await_sent(place, buf.at[:, 0, 0, pl.ds(0, 3), core], sent.at[0])
+    await_sent(place, buf.at[:, 0, pl.ds(0, 3), :, core], sent.at[1])
+    await_sent(place, buf.at[:, pl.ds(0, 3), :, :, core], sent.at[2])
+    await_sent(place, buf.at[:, :, :, :, core], sent_d)
+
+
+def fine_sems():
+    dma = pltpu.SemaphoreType.DMA
     return [dma((3, 3, 4, 2))] * 4 + [dma((3, 4, 4))] * 2
 
 
-def gather(place, buf, sems, hook=None, stepwise=False):
+def fine_gather(place, buf, sems, hook):
     send_a, recv_a, send_b, recv_b, send_d, recv_d = sems
     core = place.core
     rows = buf.shape[5]
@@ -132,8 +239,7 @@
     def line_done(j1, j2):
         for t in range(3):
             copy_d(t, j1, j2, 1 - core).wait_recv()
-        if hook is not None:
-            hook(j1, j2)
+        hook(j1, j2)
 
     thirds = range(3)
     for t in thirds:
@@ -170,34 +276,30 @@
         copy_d(t, 3, 0, core).start()
     yield
 
-    def near(j):
+    @pl.loop(0, 4)
+    def _(j):
         for t in thirds:
             for d in range(2):
                 land_a(t, 2, j, d)
                 copy_d(t, j, 2 - d, core).start()
         line_done(j, 0)
 
-    def opposite(j):
+        @pl.when(j >= 1)
+        def _():
+            line_done(j - 1, 1)
+            line_done(j - 1, 2)
+
+    line_done(3, 1)
+    line_done(3, 2)
+
+    @pl.loop(0, 4)
+    def _(j):
         for t in thirds:
             land_b(t, 2, j)
             copy_d(t, j, 3, core).start()
-        line_done(j, 1)
-        line_done(j, 2)
-        if not isinstance(j, int):
-            pl.when(j >= 1)(lambda: line_done(j - 1, 3))
-        elif j >= 1:
-            line_done(j - 1, 3)
-
-    if stepwise:
-        for step in (near, opposite):
-            for j in range(4):
-                step(j)
-                yield
-    else:
-        pl.loop(0, 4)(near)
-        pl.loop(0, 4)(opposite)
+        pl.when(j >= 1)(lambda: line_done(j - 1, 3))
+
     line_done(3, 3)
-
     for t in thirds:
         for p in range(3):
             for j in range(1 if p == 0 else 4):
@@ -276,12 +378,12 @@
 
 def main_kernel(gain, m_hbm, g_hbm, q_hbm, full, basis_ref, parts, qbuf, left_ref, lhs, norms,
                 mbuf, gbuf, part, zbuf, zown, raw, stacked, both, other,
-                ra0, rb0, ra1, rb1, ra2, rb2, pair, mix, wide,
+                ra0, rb0, ra1, rb1, ra2, rb2, pair, held, mix, wide,
                 q_sem, load_sem, z_send, z_recv, d_send, d_recv, s_send, s_recv, x_send, x_recv, n_send, n_recv, *sems):
     place = Place()
     z, x, y = place.at
     core = place.core
-    sems_q, sems_raw, sems_term = sems[:6], sems[6:12], sems[12:]
+    sems_q, sems_raw, sems_term = sems[:6], sems[6:11], sems[11:]
     count, stack_rows, width = parts.shape
     slots, _, rows, span = mbuf.shape
     chunks = width // span
@@ -321,11 +423,9 @@
     part[...] = jnp.zeros_like(part)
 
     def hook(j1, j2):
-        @pl.loop(0, 3)
-        def _(t):
+        for t in range(3):
             left, right = [], []
-            for i in range(N):
-                cz, cx, cy = place.line(t, j1, j2, i)
+            for cz, cx, cy in place.chips(t, j1, j2):
                 column = pl.multiple_of(((cz * N + cx) * N + cy) * RANK, RANK)
                 left.append(parts[t, :, pl.ds(column, RANK)])
                 right.append(qbuf[t, cz, cx, cy].reshape(RANK, RANK))
@@ -337,10 +437,10 @@
             part[t] += (small + (tile(1, 0) + tile(0, 1))) + tile(0, 0)
 
     done = 0
-    for _ in gather(place, qbuf, sems_q, hook):
+    for _ in fine_gather(place, qbuf, sems_q, hook):
         if done < chunks:
-            blend(done, min(done + 3, chunks))
-            done += 3
+            blend(done, min(done + 4, chunks))
+            done += 4
 
     quarter = rows // N
     sends = []
@@ -362,7 +462,7 @@
             zown.at[z], zown.at[z], z_send.at[1, d], z_recv.at[1, d],
             device_id=place.chip(0, d), device_id_type=MESH))
         sends[-1].start()
-    rest = gather(place, raw, sems_raw, stepwise=True)
+    rest = gather(place, raw, sems_raw)
     next(rest)
     for d in (1, 2, 3):
         spot = zown.at[place.far(0, N - d)]
@@ -377,126 +477,126 @@
 
     half = RANK // 4
 
-    def spot(t, j1, j2, whose, part=None):
+    def plane(t, distance, whose, part=None):
         where = [slice(None)] * 3
-        for p, j in ((1, j1), (2, j2)):
-            where[axis_of(t, p)] = place.far(axis_of(t, p), OFF[j])
+        where[axis_of(t, 2)] = place.far(axis_of(t, 2), distance)
         return (t, *where, whose, slice(None) if part is None else pl.ds(part * half, half))
 
-    def unit(t, j, part=None):
+    def line(t, distance, part=None):
         where = list(place.at)
-        where[axis_of(t, 0)] = place.far(axis_of(t, 0), OFF[j])
+        where[axis_of(t, 0)] = slice(None)
+        where[axis_of(t, 1)] = place.far(axis_of(t, 1), distance)
         return (t, *where, core, slice(None) if part is None else pl.ds(part * half, half))
 
-    def swap(t, j1, j2):
-        return pltpu.make_async_remote_copy(
-            full.at[spot(t, j1, j2, 1 - core)], other.at[t, j1, j2], d_send.at[t, j1, j2], d_recv.at[t, j1, j2],
-            device_id=place.sibling(), device_id_type=MESH)
-
-    def hop(t, p, d, kind, j, src, dst):
-        return pltpu.make_async_remote_copy(
-            src, dst, s_send.at[t, p, kind, j, d], s_recv.at[t, p, kind, j, d],
-            device_id=place.chip(axis_of(t, p), 1 if d == 0 else 3), device_id_type=MESH)
-
-    def far_a(t, j, d):
-        return hop(t, 2, d, 0, j, full.at[spot(t, j, 3, core, d)], ra0.at[t, d, j])
-
-    def far_b(t, j, d):
-        return hop(t, 2, d, 1, j, full.at[spot(t, j, d + 1, core)], rb0.at[t, d, j])
-
-    def mid_a(t, d):
-        return hop(t, 1, d, 0, 0, full.at[spot(t, 3, 0, core, d)], ra1.at[t, d])
-
-    def mid_b(t, d):
-        return hop(t, 1, d, 1, 0, full.at[spot(t, d + 1, 0, core)], rb1.at[t, d])
-
-    def end_a(t, d):
-        return hop(t, 0, d, 0, 0, full.at[unit(t, 3, d)], ra2.at[t, d])
-
-    def end_b(t, d):
-        return hop(t, 0, d, 1, 0, full.at[unit(t, d + 1)], rb2.at[t, d])
-
-    def multiply(j1, j2):
+    def unit(t, distance, part=None):
+        where = list(place.at)
+        where[axis_of(t, 0)] = place.far(axis_of(t, 0), distance)
+        return (t, *where, core, slice(None) if part is None else pl.ds(part * half, half))
+
+    spots = (plane, line, unit)
+    went = (1, 3)
+    first, whole = (ra0, ra1, ra2), (rb0, rb1, rb2)
+
+    def swap(t, n, distance):
+        where = plane(t, distance, 1 - core)
+        pltpu.make_async_remote_copy(
+            full.at[where], other.at[where[:4]], d_send, d_recv.at[n],
+            device_id=place.sibling(), device_id_type=MESH).start()
+
+    def block(t, step, distance, part=None):
+        return plane(t, distance, core, part) if step == 0 else spots[step](t, distance, part)
+
+    def start(step, kind, d):
+        for t in range(3):
+            src = block(t, step, 2, d) if kind == 0 else block(t, step, went[d])
+            dst = (first, whole)[kind][step].at[t, d]
+            pltpu.make_async_remote_copy(
+                full.at[src], dst, s_send.at[step, kind], s_recv.at[step, kind, d],
+                device_id=place.chip(axis_of(t, 2 - step), 1 if d == 0 else 3), device_id_type=MESH).start()
+
+    def take_first(step, d):
+        await_landed(place, first[step].at[:, d], s_recv.at[step, 0, d])
+        for t in range(3):
+            here = block(t, step, went[d], d)
+            full[here] = full[here] + first[step][t, d]
+        start(step, 1, d)
+
+    def take_whole(step):
+        for d in range(2):
+            await_landed(place, whole[step].at[:, d], s_recv.at[step, 1, d])
+        for t in range(3):
+            here = block(t, step, 0)
+            full[here] = full[here] + (whole[step][t, 0] + whole[step][t, 1])
+
+    def multiply(t, middle, distance):
+        where = [place.line(t, middle, distance, c) for c in range(N)]
+        right = [parts[t, :, pl.ds(pl.multiple_of(((cz * N + cx) * N + cy) * RANK, RANK), RANK)] for cz, cx, cy in where]
+        right = jnp.concatenate(right, 1)
+        out = dot(stacked[t], jnp.concatenate([right, right[:rows]], 0))
+        out = out[:RANK] + out[RANK:]
+        for c, (cz, cx, cy) in enumerate(where):
+            full[t, cz, cx, cy] = out[:, c * RANK:(c + 1) * RANK].reshape(2, RANK // 2, RANK)
+
+    def multiply_plane(n, distance):
         @pl.loop(0, 3)
         def _(t):
-            where = [place.line(t, j1, j2, i) for i in range(N)]
-            right = [parts[t, :, pl.ds(pl.multiple_of(((cz * N + cx) * N + cy) * RANK, RANK), RANK)] for cz, cx, cy in where]
-            right = jnp.concatenate(right, 1)
-            out = dot(stacked[t], jnp.concatenate([right, right[:rows]], 0))
-            out = out[:RANK] + out[RANK:]
-            for i, (cz, cx, cy) in enumerate(where):
-                full[t, cz, cx, cy] = out[:, i * RANK:(i + 1) * RANK].reshape(2, RANK // 2, RANK)
-        for t in range(3):
-            swap(t, j1, j2).start()
-
-    def settle(j1, j2):
-        for t in range(3):
-            swap(t, j1, j2).wait_recv()
-            here = spot(t, j1, j2, core)
-            full[here] = full[here] + other[t, j1, j2]
-            if j2 == 3:
-                for d in range(2):
-                    far_a(t, j1, d).start()
-            elif j2 > 0:
-                d = j2 - 1
-                far_a(t, j1, d).wait_recv()
-                here = spot(t, j1, j2, core, d)
-                full[here] = full[here] + ra0[t, d, j1]
-                far_b(t, j1, d).start()
-
-    lines = [(j1, j2) for j2 in (3, 2, 1, 0) for j1 in (3, 2, 1, 0)]
-    for i, line in enumerate(lines):
-        multiply(*line)
-        if i:
-            settle(*lines[i - 1])
-        next(rest, None)
-    settle(*lines[-1])
+            for middle in range(N):
+                multiply(t, middle, distance)
+        for t in range(3):
+            swap(t, n, distance)
+
+    def settle(n, distance):
+        await_landed(place, other.at[:, 0], d_recv.at[n])
+
+        @pl.loop(0, 3 * N)
+        def _(i):
+            t, middle = i // N, lax.rem(i, N)
+            for c in range(N):
+                cz, cx, cy = place.line(t, middle, distance, c)
+                full[t, cz, cx, cy, core] += other[t, cz, cx, cy]
+
+    order = (2, 3, 1, 0)
+    multiply_plane(0, 2)
+    next(rest, None)
+    next(rest, None)
+    multiply_plane(1, 3)
+    settle(0, 2)
+    start(0, 0, 0)
+    start(0, 0, 1)
+    next(rest, None)
+    multiply_plane(2, 1)
+    next(rest, None)
+    settle(1, 3)
     for _ in rest:
         pass
+    take_first(0, 1)
+    settle(2, 1)
+    take_first(0, 0)
 
     def ring_ends():
-        for j in (3, 2, 1, 0):
-            for t in range(3):
-                here = spot(t, j, 0, core)
-                for d in range(2):
-                    far_b(t, j, d).wait_recv()
-                full[here] = full[here] + (rb0[t, 0, j] + rb0[t, 1, j])
-                if j == 3:
-                    for d in range(2):
-                        mid_a(t, d).start()
-        yield
-        for t in range(3):
-            for d in range(2):
-                mid_a(t, d).wait_recv()
-                here = spot(t, d + 1, 0, core, d)
-                full[here] = full[here] + ra1[t, d]
-                mid_b(t, d).start()
-        yield
-        for t in range(3):
-            here = spot(t, 0, 0, core)
-            for d in range(2):
-                mid_b(t, d).wait_recv()
-            full[here] = full[here] + (rb1[t, 0] + rb1[t, 1])
-            for d in range(2):
-                end_a(t, d).start()
-        yield
-        for t in range(3):
-            for d in range(2):
-                end_a(t, d).wait_recv()
-                here = unit(t, d + 1, d)
-                full[here] = full[here] + ra2[t, d]
-                end_b(t, d).start()
-        yield
-        for t in range(3):
-            here = unit(t, 0)
-            for d in range(2):
-                end_b(t, d).wait_recv()
-            pair[t, core] = full[here] + (rb2[t, 0] + rb2[t, 1])
+        take_whole(0)
+        start(1, 0, 0)
+        start(1, 0, 1)
+        yield
+        take_first(1, 0)
+        take_first(1, 1)
+        yield
+        take_whole(1)
+        start(2, 0, 0)
+        start(2, 0, 1)
+        yield
+        take_first(2, 0)
+        take_first(2, 1)
+        yield
+        take_whole(2)
+        for t in range(3):
+            held[t] = full[unit(t, 0)]
+            pair[t, core] = held[t]
         half_swap.start()
         yield
 
     half_swap = pltpu.make_async_remote_copy(
-        pair.at[:, core], pair.at[:, core], x_send, x_recv, device_id=place.sibling(), device_id_type=MESH)
+        held, pair.at[:, core], x_send, x_recv, device_id=place.sibling(), device_id_type=MESH)
 
     def grams(inverse):
         if inverse:
@@ -526,50 +626,54 @@
 
     grams(False)
     ends = ring_ends()
-    for i in range(0, 8, 2):
-        pl.loop(i, i + 2)(lambda i: factor_block(both, i))
-        next(ends)
+
+    @pl.loop(0, N)
+    def _(i):
+        for t in range(3):
+            multiply(t, i, 0)
+        factor_block(both, i)
+
+    for t in range(3):
+        swap(t, 3, 0)
+    pl.loop(N, 8)(lambda i: factor_block(both, i))
+    settle(3, 0)
+    next(ends)
     for t in range(3):
         mix[t] = both[t, :, RANK:]
     grams(True)
+    for i in (0, 2, 4):
+        next(ends)
+        pl.loop(i, i + 2)(lambda i: factor_block(both, i))
     next(ends)
-    pl.loop(0, 8)(lambda i: factor_block(both, i))
+    factor_block(both, 6)
+    await_landed(place, pair.at[:, 1 - core], x_recv)
     for t in range(3):
-        left = dot(zown[:, t].reshape(rows, RANK), mix[t], NT, HIGH)
-        inv = both[t, :, RANK:]
-        left_ref[t] = dot(left, inv, NT, HIGH)
-        mix[t] = dot(inv, mix[t], precision=HIGH) * (1.0 / N)
-    pltpu.make_async_remote_copy(
-        pair.at[:, 1 - core], pair.at[:, 1 - core], x_send, x_recv, device_id=place.sibling(),
-        device_id_type=MESH).wait_recv()
+        pair[t] = dot(mix[t] * (1.0 / N), pair[t].reshape(RANK, RANK), precision=HIGH).reshape(2, RANK // 2, RANK)
+    factor_block(both, 7)
     half_swap.wait_send()
     for send in sends:
         send.wait_send()
-    for t in range(3):
-        for d in range(2):
-            for j in range(N):
-                far_a(t, j, d).wait_send()
-                far_b(t, j, d).wait_send()
-            for copy in (mid_a, mid_b, end_a, end_b):
-                copy(t, d).wait_send()
-        for j1, j2 in lines:
-            swap(t, j1, j2).wait_send()
+    for step in range(3):
+        await_sent(place, first[step], s_send.at[step, 0])
+        await_sent(place, whole[step], s_send.at[step, 1])
+    await_sent(place, other, d_send)
 
     term = qbuf
     mine = pl.ds(pl.multiple_of(core * (RANK // 2), RANK // 2), RANK // 2)
     ones = jnp.ones((8, RANK), F32)
     own = lax.broadcasted_iota(jnp.int32, (RANK, RANK), 0) // (RANK // 2) == core
     for t in range(3):
-        whole = dot(mix[t], pair[t].reshape(RANK, RANK), precision=HIGH)
-        pair[t] = whole.reshape(2, RANK // 2, RANK)
+        pair[t] = dot(both[t, :, RANK:], pair[t].reshape(RANK, RANK), precision=HIGH).reshape(2, RANK // 2, RANK)
         term[t, z, x, y, core] = pair[t, core]
-        norms[0, core, t] = dot(ones, jnp.where(own, whole * whole, 0.0), NT, HIGH)
 
     def tell(stage, where, peer, sem):
         return pltpu.make_async_remote_copy(norms.at[stage, where], norms.at[stage, where], n_send.at[stage, sem],
                                             n_recv.at[stage, sem], device_id=peer, device_id_type=MESH)
 
     def sum_norms():
+        for t in range(3):
+            product = pair[t].reshape(RANK, RANK)
+            norms[0, core, t] = dot(ones, jnp.where(own, product * product, 0.0), NT, HIGH)
         tell(0, core, place.sibling(), 0).start()
         yield
         tell(0, 1 - core, place.sibling(), 0).wait_recv()
@@ -584,6 +688,10 @@
             for d in (1, 2, 3):
                 tell(stage, place.far(axis, N - d), place.chip(axis, d), d).wait_recv()
             total = (norms[stage, 0] + norms[stage, 1]) + (norms[stage, 2] + norms[stage, 3])
+            if axis == 0:
+                for t in range(3):
+                    left = dot(zown[:, t].reshape(rows, RANK), mix[t], NT, HIGH)
+                    left_ref[t] = dot(left, both[t, :, RANK:], NT, HIGH)
         scales = 1.0 / jnp.sqrt(total + 1e-6)
         for t in range(3):
             scale = scales[t, 0:1]
@@ -600,22 +708,20 @@
         yield
 
     def emit(j1, j2):
-        @pl.loop(0, 3)
-        def _(t):
-            where = [place.line(t, j1, j2, i) for i in range(N)]
-            block = jnp.concatenate([term[t, cz, cx, cy].reshape(RANK, RANK) for cz, cx, cy in where], 1)
+        for t in range(3):
+            where = place.chips(t, j1, j2)
+            block = jnp.concatenate([term[(t, *chip)].reshape(RANK, RANK) for chip in where], 1)
             out = dot(lhs[t], jnp.concatenate(split(block, 2), 0))
             out = out[:RANK] + out[RANK:]
             for i, (cz, cx, cy) in enumerate(where):
                 column = pl.ds(pl.multiple_of(((cz * N + cx) * N + cy) * RANK, RANK), RANK)
                 tile = slice(i * RANK, (i + 1) * RANK)
-                h, m, l = [parts[t, k * rows:(k + 1) * rows, column].astype(F32) for k in range(3)]
+                h, m, l = [parts[t, j * rows:(j + 1) * rows, column].astype(F32) for j in range(3)]
                 full[t, cz, cx, cy, 0] = (h + (m + l)) - out[:rows, tile]
                 full[t, cz, cx, cy, 1] = out[rows:, tile]
 
     norm_steps = sum_norms()
-    next(norm_steps)
-    for _ in gather(place, term, sems_term, emit):
+    for _ in fine_gather(place, term, sems_term, emit):
         next(norm_steps, None)
 
 
@@ -654,10 +760,10 @@
             room(3, 2, N, N, 32, RANK), room(3, 2, N, N, 64, RANK),
             room(3, 2, N, 32, RANK), room(3, 2, N, 64, RANK),
             room(3, 2, 32, RANK), room(3, 2, 64, RANK),
-            room(3, 2, 64, RANK), room(3, RANK, RANK),
+            room(3, 2, 64, RANK), room(3, 64, RANK), room(3, RANK, RANK),
             pltpu.VMEM((3, 2 * RANK, 3 * RANK), BF16),
             dma((3,)), dma((2, 4)), dma((2, 4)), dma((2, 4)),
-            dma((3, N, N)), dma((3, N, N)), dma((3, 3, 2, N, 2)), dma((3, 3, 2, N, 2)), dma, dma, dma((4, 4)), dma((4, 4))] + gather_sems() * 3,
+            dma, dma((N,)), dma((3, 2)), dma((3, 2, 2)), dma, dma, dma((4, 4)), dma((4, 4))] + fine_sems() + gather_sems() + fine_sems(),
         compiler_params=pltpu.CompilerParams(collective_id=0, has_side_effects=True, vmem_limit_bytes=49 * 2 ** 20),
     )(momentum, gradient, basis)
     span = 2048

time: 173 us -> 157 us (0.908)
  Pallas kernels: 173 us -> 156 us
    pallas_call x1, Pallas kernels: 166 us -> 149 us  [body(): pl.pallas_call(functools.partial(main_kernel, gain), name='dion', out_sha...]
where the time goes in v4:
time: 157 us
  Pallas kernels  156 us (99%)
    pallas_call x1, Pallas kernels, body(): pl.pallas_call(functools.partial(main_kernel, gain), name='dion', out_sha...  149 us
    pallas_call x1, Pallas kernels, body(): pl.pallas_call(last_kernel, name='outputs', grid=(3, width // span), out_...  7.07 us

profile of v4, /device:TPU:1, one launch (start us, length us, event | category | flops | bytes accessed | tf_op | source)
XLA Modules:
  0.0 156.6 jit_solution(1129370707871142950)
XLA Ops:
  0.6 148.9 %dion.1 = (f32[3,4,4,4,2,64,128]{6,5,4,3,2,1,0:T(8,128)S(1)}, f32[64,384]{1,0:T(8,128)S(1)}) custom-call(f32[3,64,8192]{2,1,0:T(8,128)} %bitcast.2, f32[3,64,8192]{2,1,0:T(8,128)} %bitcast.3, f32[64,384]{1,0:T(8,128)} %q_hbm.1), custom_call_target="tpu_custom_call" | custom-call | tf_op jit(solution)/shard_map/dion/pallas_call | solution.py:747
  149.5 7.1 %outputs.1 = (f32[1,3,64,8192]{3,2,1,0:T(8,128)}, f32[3,64,8192]{2,1,0:T(8,128)}, f32[64,384]{1,0:T(8,128)}) custom-call(f32[3,4,4,4,2,64,128]{6,5,4,3,2,1,0:T(8,128)S(1)} %get-tuple-element.5.both_ref, f32[64,384]{1,0:T(8,128)S(1)} %get-tuple-element.6.basis_in), custom_call_target="tpu_custom_call" | custom-call | tf_op jit(solution)/shard_map/outputs/pallas_call | solution.py:771

commit v5 on v4

--- a/solution.py
+++ b/solution.py
@@ -378,8 +378,8 @@
 
 def main_kernel(gain, m_hbm, g_hbm, q_hbm, full, basis_ref, parts, qbuf, left_ref, lhs, norms,
                 mbuf, gbuf, part, zbuf, zown, raw, stacked, both, other,
-                ra0, rb0, ra1, rb1, ra2, rb2, pair, held, mix, wide,
-                q_sem, load_sem, z_send, z_recv, d_send, d_recv, s_send, s_recv, x_send, x_recv, n_send, n_recv, *sems):
+                ra0, rb0, ra1, rb1, ra2, rb2, pair, held, mix, sums, wide,
+                q_sem, load_sem, z_send, z_recv, d_send, d_recv, s_send, s_recv, x_send, x_recv, g_send, g_recv, n_send, n_recv, *sems):
     place = Place()
     z, x, y = place.at
     core = place.core
@@ -439,8 +439,8 @@
     done = 0
     for _ in fine_gather(place, qbuf, sems_q, hook):
         if done < chunks:
-            blend(done, min(done + 4, chunks))
-            done += 4
+            blend(done, min(done + 2, chunks))
+            done += 2
 
     quarter = rows // N
     sends = []
@@ -604,11 +604,13 @@
                 h, m, l = split(mix[t].T, 3)
                 wide[t] = jnp.concatenate([jnp.concatenate([h, m, l], 1), jnp.concatenate([m, h, h], 1)], 0)
 
+        first, many = (core * 2, 2) if inverse else (0, N)
+
         def add(i, grams):
             out = []
             for t in range(3):
                 whole, low = grams[t]
-                some = raw[t, i].reshape(512, RANK)
+                some = raw[t, first + i].reshape(512, RANK)
                 if inverse:
                     h, m, l = split(some, 3)
                     main = dot(jnp.concatenate([h, m], 1), wide[t, :, :2 * RANK])
@@ -620,9 +622,19 @@
             return tuple(out)
 
         zero = jnp.zeros((RANK, RANK), F32)
-        for t, (whole, low) in enumerate(lax.fori_loop(0, N, add, ((zero, zero),) * 3)):
-            both[t, :, :RANK] = whole + (low + low.T)
+        for t, (whole, low) in enumerate(lax.fori_loop(0, many, add, ((zero, zero),) * 3)):
             both[t, :, RANK:] = eye
+            if inverse:
+                sums[0, t] = whole + (low + low.T)
+            else:
+                both[t, :, :RANK] = whole + (low + low.T)
+        if inverse:
+            trade = pltpu.make_async_remote_copy(sums.at[0], sums.at[1], g_send, g_recv, device_id=place.sibling(),
+                                                 device_id_type=MESH)
+            trade.start()
+            trade.wait()
+            for t in range(3):
+                both[t, :, :RANK] = sums[0, t] + sums[1, t]
 
     grams(False)
     ends = ring_ends()
@@ -760,13 +772,13 @@
             room(3, 2, N, N, 32, RANK), room(3, 2, N, N, 64, RANK),
             room(3, 2, N, 32, RANK), room(3, 2, N, 64, RANK),
             room(3, 2, 32, RANK), room(3, 2, 64, RANK),
-            room(3, 2, 64, RANK), room(3, 64, RANK), room(3, RANK, RANK),
+            room(3, 2, 64, RANK), room(3, 64, RANK), room(3, RANK, RANK), room(2, 3, RANK, RANK),
             pltpu.VMEM((3, 2 * RANK, 3 * RANK), BF16),
             dma((3,)), dma((2, 4)), dma((2, 4)), dma((2, 4)),
-            dma, dma((N,)), dma((3, 2)), dma((3, 2, 2)), dma, dma, dma((4, 4)), dma((4, 4))] + fine_sems() + gather_sems() + fine_sems(),
+            dma, dma((N,)), dma((3, 2)), dma((3, 2, 2)), dma, dma, dma, dma, dma((4, 4)), dma((4, 4))] + fine_sems() + gather_sems() + fine_sems(),
         compiler_params=pltpu.CompilerParams(collective_id=0, has_side_effects=True, vmem_limit_bytes=49 * 2 ** 20),
     )(momentum, gradient, basis)
-    span = 2048
+    span = 4096
     full, basis_next = [pltpu.with_memory_space_constraint(a, pltpu.VMEM) for a in (full, basis_next)]
     return pl.pallas_call(
         last_kernel,

time: 157 us -> 154 us (0.981)
  Pallas kernels: 156 us -> 154 us
where the time goes in v5:
time: 154 us
  Pallas kernels  154 us (100%)
    pallas_call x1, Pallas kernels, body(): pl.pallas_call(functools.partial(main_kernel, gain), name='dion', out_sha...  148 us
    pallas_call x1, Pallas kernels, body(): pl.pallas_call(last_kernel, name='outputs', grid=(3, width // span), out_...  5.61 us

profile of v5, /device:TPU:1, one launch (start us, length us, event | category | flops | bytes accessed | tf_op | source)
XLA Modules:
  0.0 154.3 jit_solution(2872397320640811684)
XLA Ops:
  0.6 148.1 %dion.1 = (f32[3,4,4,4,2,64,128]{6,5,4,3,2,1,0:T(8,128)S(1)}, f32[64,384]{1,0:T(8,128)S(1)}) custom-call(f32[3,64,8192]{2,1,0:T(8,128)} %bitcast.2, f32[3,64,8192]{2,1,0:T(8,128)} %bitcast.3, f32[64,384]{1,0:T(8,128)} %q_hbm.1), custom_call_target="tpu_custom_call" | custom-call | tf_op jit(solution)/shard_map/dion/pallas_call | solution.py:759
  148.7 5.6 %outputs.1 = (f32[1,3,64,8192]{3,2,1,0:T(8,128)}, f32[3,64,8192]{2,1,0:T(8,128)}, f32[64,384]{1,0:T(8,128)}) custom-call(f32[3,4,4,4,2,64,128]{6,5,4,3,2,1,0:T(8,128)S(1)} %get-tuple-element.5.both_ref, f32[64,384]{1,0:T(8,128)S(1)} %get-tuple-element.6.basis_in), custom_call_target="tpu_custom_call" | custom-call | tf_op jit(solution)/shard_map/outputs/pallas_call | solution.py:783

commit v6 on v4

--- a/solution.py
+++ b/solution.py
@@ -378,8 +378,8 @@
 
 def main_kernel(gain, m_hbm, g_hbm, q_hbm, full, basis_ref, parts, qbuf, left_ref, lhs, norms,
                 mbuf, gbuf, part, zbuf, zown, raw, stacked, both, other,
-                ra0, rb0, ra1, rb1, ra2, rb2, pair, held, mix, wide,
-                q_sem, load_sem, z_send, z_recv, d_send, d_recv, s_send, s_recv, x_send, x_recv, n_send, n_recv, *sems):
+                ra0, rb0, ra1, rb1, ra2, rb2, pair, held, inv, wide,
+                q_sem, load_sem, z_send, z_recv, d_send, d_recv, s_send, s_recv, x_send, x_recv, g_send, g_recv, n_send, n_recv, *sems):
     place = Place()
     z, x, y = place.at
     core = place.core
@@ -439,8 +439,8 @@
     done = 0
     for _ in fine_gather(place, qbuf, sems_q, hook):
         if done < chunks:
-            blend(done, min(done + 4, chunks))
-            done += 4
+            blend(done, min(done + 2, chunks))
+            done += 2
 
     quarter = rows // N
     sends = []
@@ -598,31 +598,42 @@
     half_swap = pltpu.make_async_remote_copy(
         held, pair.at[:, core], x_send, x_recv, device_id=place.sibling(), device_id_type=MESH)
 
+    mine_k = lax.rem(z, 3)
+
     def grams(inverse):
         if inverse:
-            for t in range(3):
-                h, m, l = split(mix[t].T, 3)
-                wide[t] = jnp.concatenate([jnp.concatenate([h, m, l], 1), jnp.concatenate([m, h, h], 1)], 0)
+            h, m, l = split(inv[0, z].T, 3)
+            wide[...] = jnp.concatenate([jnp.concatenate([h, m, l], 1), jnp.concatenate([m, h, h], 1)], 0)
 
         def add(i, grams):
-            out = []
-            for t in range(3):
-                whole, low = grams[t]
-                some = raw[t, i].reshape(512, RANK)
-                if inverse:
-                    h, m, l = split(some, 3)
-                    main = dot(jnp.concatenate([h, m], 1), wide[t, :, :2 * RANK])
-                    rest = dot(jnp.concatenate([h, l], 1), wide[t, :, 2 * RANK:])
-                    some = main[:, :RANK] + (main[:, RANK:] + rest)
-                all_ = dot(jnp.concatenate(split(some.T, 3), 0), jnp.concatenate(split(some, 2), 1))
-                tile = lambda i, j: all_[i * RANK:(i + 1) * RANK, j * RANK:(j + 1) * RANK]
-                out.append((whole + (tile(0, 0) + ((tile(0, 1) + tile(1, 0)) + tile(1, 1))), low + tile(2, 0)))
-            return tuple(out)
+            whole, low = grams
+            some = raw[mine_k, i].reshape(512, RANK)
+            if inverse:
+                h, m, l = split(some, 3)
+                main = dot(jnp.concatenate([h, m], 1), wide[:, :2 * RANK])
+                rest = dot(jnp.concatenate([h, l], 1), wide[:, 2 * RANK:])
+                some = main[:, :RANK] + (main[:, RANK:] + rest)
+            all_ = dot(jnp.concatenate(split(some.T, 3), 0), jnp.concatenate(split(some, 2), 1))
+            tile = lambda i, j: all_[i * RANK:(i + 1) * RANK, j * RANK:(j + 1) * RANK]
+            return whole + (tile(0, 0) + ((tile(0, 1) + tile(1, 0)) + tile(1, 1))), low + tile(2, 0)
 
         zero = jnp.zeros((RANK, RANK), F32)
-        for t, (whole, low) in enumerate(lax.fori_loop(0, N, add, ((zero, zero),) * 3)):
-            both[t, :, :RANK] = whole + (low + low.T)
-            both[t, :, RANK:] = eye
+        whole, low = lax.fori_loop(0, N, add, (zero, zero))
+        both[0, :, :RANK] = whole + (low + low.T)
+        both[0, :, RANK:] = eye
+
+    def pass_on(sweep, d, whose):
+        return pltpu.make_async_remote_copy(inv.at[sweep, whose], inv.at[sweep, whose], g_send.at[sweep, d],
+                                            g_recv.at[sweep, d], device_id=place.chip(0, d), device_id_type=MESH)
+
+    def publish(sweep):
+        inv[sweep, z] = both[0, :, RANK:]
+        for d in (1, 2, 3):
+            pass_on(sweep, d, z).start()
+
+    def learn(sweep):
+        for d in (1, 2, 3):
+            pass_on(sweep, d, place.far(0, N - d)).wait_recv()
 
     grams(False)
     ends = ring_ends()
@@ -638,8 +649,7 @@
     pl.loop(N, 8)(lambda i: factor_block(both, i))
     settle(3, 0)
     next(ends)
-    for t in range(3):
-        mix[t] = both[t, :, RANK:]
+    publish(0)
     grams(True)
     for i in (0, 2, 4):
         next(ends)
@@ -647,9 +657,11 @@
     next(ends)
     factor_block(both, 6)
     await_landed(place, pair.at[:, 1 - core], x_recv)
+    learn(0)
     for t in range(3):
-        pair[t] = dot(mix[t] * (1.0 / N), pair[t].reshape(RANK, RANK), precision=HIGH).reshape(2, RANK // 2, RANK)
+        pair[t] = dot(inv[0, t] * (1.0 / N), pair[t].reshape(RANK, RANK), precision=HIGH).reshape(2, RANK // 2, RANK)
     factor_block(both, 7)
+    publish(1)
     half_swap.wait_send()
     for send in sends:
         send.wait_send()
@@ -658,12 +670,14 @@
         await_sent(place, whole[step], s_send.at[step, 1])
     await_sent(place, other, d_send)
 
+    learn(1)
+
     term = qbuf
     mine = pl.ds(pl.multiple_of(core * (RANK // 2), RANK // 2), RANK // 2)
     ones = jnp.ones((8, RANK), F32)
     own = lax.broadcasted_iota(jnp.int32, (RANK, RANK), 0) // (RANK // 2) == core
     for t in range(3):
-        pair[t] = dot(both[t, :, RANK:], pair[t].reshape(RANK, RANK), precision=HIGH).reshape(2, RANK // 2, RANK)
+        pair[t] = dot(inv[1, t], pair[t].reshape(RANK, RANK), precision=HIGH).reshape(2, RANK // 2, RANK)
         term[t, z, x, y, core] = pair[t, core]
 
     def tell(stage, where, peer, sem):
@@ -690,8 +704,8 @@
             total = (norms[stage, 0] + norms[stage, 1]) + (norms[stage, 2] + norms[stage, 3])
             if axis == 0:
                 for t in range(3):
-                    left = dot(zown[:, t].reshape(rows, RANK), mix[t], NT, HIGH)
-                    left_ref[t] = dot(left, both[t, :, RANK:], NT, HIGH)
+                    left = dot(zown[:, t].reshape(rows, RANK), inv[0, t], NT, HIGH)
+                    left_ref[t] = dot(left, inv[1, t], NT, HIGH)
         scales = 1.0 / jnp.sqrt(total + 1e-6)
         for t in range(3):
             scale = scales[t, 0:1]
@@ -701,6 +715,9 @@
                 [jnp.concatenate([high, high], 1), jnp.concatenate([low, jnp.zeros_like(low)], 1)], 0)
             basis = pair[t].reshape(RANK, RANK).T * scale
             basis_ref[:, t * RANK:(t + 1) * RANK] = jnp.where(core == 0, basis[:RANK // 2], basis[RANK // 2:])
+        for sweep in range(2):
+            for d in (1, 2, 3):
+                pass_on(sweep, d, z).wait_send()
         tell(0, core, place.sibling(), 0).wait_send()
         for axis in range(3):
             for d in (1, 2, 3):
@@ -755,18 +772,18 @@
             pltpu.VMEM((3, 2 * RANK, 2 * RANK), BF16), room(4, N, 3, 8, RANK),
             room(4, count, rows, 512), room(4, count, rows, 512),
             room(count, rows, RANK), room(N, 3, 16, RANK), room(N, 3, 16, RANK), room(3, *chips, 16, RANK),
-            pltpu.VMEM((3, 2 * RANK, 4 * rows), BF16), room(3, RANK, 2 * RANK),
+            pltpu.VMEM((3, 2 * RANK, 4 * rows), BF16), room(1, RANK, 2 * RANK),
             room(3, N, N, N, 64, RANK),
             room(3, 2, N, N, 32, RANK), room(3, 2, N, N, 64, RANK),
             room(3, 2, N, 32, RANK), room(3, 2, N, 64, RANK),
             room(3, 2, 32, RANK), room(3, 2, 64, RANK),
-            room(3, 2, 64, RANK), room(3, 64, RANK), room(3, RANK, RANK),
-            pltpu.VMEM((3, 2 * RANK, 3 * RANK), BF16),
+            room(3, 2, 64, RANK), room(3, 64, RANK), room(2, N, RANK, RANK),
+            pltpu.VMEM((2 * RANK, 3 * RANK), BF16),
             dma((3,)), dma((2, 4)), dma((2, 4)), dma((2, 4)),
-            dma, dma((N,)), dma((3, 2)), dma((3, 2, 2)), dma, dma, dma((4, 4)), dma((4, 4))] + fine_sems() + gather_sems() + fine_sems(),
+            dma, dma((N,)), dma((3, 2)), dma((3, 2, 2)), dma, dma, dma((2, 4)), dma((2, 4)), dma((4, 4)), dma((4, 4))] + fine_sems() + gather_sems() + fine_sems(),
         compiler_params=pltpu.CompilerParams(collective_id=0, has_side_effects=True, vmem_limit_bytes=49 * 2 ** 20),
     )(momentum, gradient, basis)
-    span = 2048
+    span = 4096
     full, basis_next = [pltpu.with_memory_space_constraint(a, pltpu.VMEM) for a in (full, basis_next)]
     return pl.pallas_call(
         last_kernel,

time: 157 us -> 160 us (1.019)
  Pallas kernels: 156 us -> 159 us
    pallas_call x1, Pallas kernels: 149 us -> 154 us  [body(): pl.pallas_call(functools.partial(main_kernel, gain), name='dion', out_sha...]
where the time goes in v6:
time: 160 us
  Pallas kernels  159 us (99%)
    pallas_call x1, Pallas kernels, body(): pl.pallas_call(functools.partial(main_kernel, gain), name='dion', out_sha...  154 us
    pallas_call x1, Pallas kernels, body(): pl.pallas_call(last_kernel, name='outputs', grid=(3, width // span), out_...  5.61 us

profile of v6, /device:TPU:1, one launch (start us, length us, event | category | flops | bytes accessed | tf_op | source)
XLA Modules:
  0.0 160.1 jit_solution(13384157369092363158)
XLA Ops:
  0.6 153.8 %dion.1 = (f32[3,4,4,4,2,64,128]{6,5,4,3,2,1,0:T(8,128)S(1)}, f32[64,384]{1,0:T(8,128)S(1)}) custom-call(f32[3,64,8192]{2,1,0:T(8,128)} %bitcast.2, f32[3,64,8192]{2,1,0:T(8,128)} %bitcast.3, f32[64,384]{1,0:T(8,128)} %q_hbm.1), custom_call_target="tpu_custom_call" | custom-call | tf_op jit(solution)/shard_map/dion/pallas_call | solution.py:764
  154.4 5.6 %outputs.1 = (f32[1,3,64,8192]{3,2,1,0:T(8,128)}, f32[3,64,8192]{2,1,0:T(8,128)}, f32[64,384]{1,0:T(8,128)}) custom-call(f32[3,4,4,4,2,64,128]{6,5,4,3,2,1,0:T(8,128)S(1)} %get-tuple-element.5.both_ref, f32[64,384]{1,0:T(8,128)S(1)} %get-tuple-element.6.basis_in), custom_call_target="tpu_custom_call" | custom-call | tf_op jit(solution)/shard_map/outputs/pallas_call | solution.py:788

commit v7 on v5

--- a/solution.py
+++ b/solution.py
@@ -538,12 +538,13 @@
             full[t, cz, cx, cy] = out[:, c * RANK:(c + 1) * RANK].reshape(2, RANK // 2, RANK)
 
     def multiply_plane(n, distance):
-        @pl.loop(0, 3)
-        def _(t):
-            for middle in range(N):
-                multiply(t, middle, distance)
-        for t in range(3):
+        for t in range(3):
+            @pl.loop(0, 2)
+            def _(i):
+                multiply(t, 2 * i, distance)
+                multiply(t, 2 * i + 1, distance)
             swap(t, n, distance)
+            next(rest, None)
 
     def settle(n, distance):
         await_landed(place, other.at[:, 0], d_recv.at[n])
@@ -557,21 +558,13 @@
 
     order = (2, 3, 1, 0)
     multiply_plane(0, 2)
-    next(rest, None)
-    next(rest, None)
     multiply_plane(1, 3)
     settle(0, 2)
     start(0, 0, 0)
     start(0, 0, 1)
-    next(rest, None)
-    multiply_plane(2, 1)
-    next(rest, None)
-    settle(1, 3)
     for _ in rest:
         pass
-    take_first(0, 1)
-    settle(2, 1)
-    take_first(0, 0)
+    settle(1, 3)
 
     def ring_ends():
         take_whole(0)
@@ -639,29 +632,37 @@
     grams(False)
     ends = ring_ends()
 
-    @pl.loop(0, N)
-    def _(i):
-        for t in range(3):
-            multiply(t, i, 0)
-        factor_block(both, i)
-
+    def beside(low, high, distance, shift):
+        @pl.loop(low, high)
+        def _(i):
+            for t in range(3):
+                multiply(t, i, distance)
+            factor_block(both, i + shift)
+
+    beside(0, N, 1, 0)
+    for t in range(3):
+        swap(t, 2, 1)
+    take_first(0, 1)
+    beside(0, 2, 0, N)
+    settle(2, 1)
+    take_first(0, 0)
+    beside(2, N, 0, N)
     for t in range(3):
         swap(t, 3, 0)
-    pl.loop(N, 8)(lambda i: factor_block(both, i))
-    settle(3, 0)
-    next(ends)
     for t in range(3):
         mix[t] = both[t, :, RANK:]
     grams(True)
+    settle(3, 0)
     for i in (0, 2, 4):
         next(ends)
         pl.loop(i, i + 2)(lambda i: factor_block(both, i))
     next(ends)
     factor_block(both, 6)
+    next(ends)
+    factor_block(both, 7)
     await_landed(place, pair.at[:, 1 - core], x_recv)
     for t in range(3):
         pair[t] = dot(mix[t] * (1.0 / N), pair[t].reshape(RANK, RANK), precision=HIGH).reshape(2, RANK // 2, RANK)
-    factor_block(both, 7)
     half_swap.wait_send()
     for send in sends:
         send.wait_send()

time: 154 us -> 160 us (1.039)
  Pallas kernels: 154 us -> 159 us
    pallas_call x1, Pallas kernels: 148 us -> 154 us  [body(): pl.pallas_call(functools.partial(main_kernel, gain), name='dion', out_sha...]
where the time goes in v7:
time: 160 us
  Pallas kernels  159 us (99%)
    pallas_call x1, Pallas kernels, body(): pl.pallas_call(functools.partial(main_kernel, gain), name='dion', out_sha...  154 us
    pallas_call x1, Pallas kernels, body(): pl.pallas_call(last_kernel, name='outputs', grid=(3, width // span), out_...  5.61 us

profile of v7, /device:TPU:1, one launch (start us, length us, event | category | flops | bytes accessed | tf_op | source)
XLA Modules:
  0.0 159.8 jit_solution(1639146713076892212)
XLA Ops:
  0.6 153.5 %dion.1 = (f32[3,4,4,4,2,64,128]{6,5,4,3,2,1,0:T(8,128)S(1)}, f32[64,384]{1,0:T(8,128)S(1)}) custom-call(f32[3,64,8192]{2,1,0:T(8,128)} %bitcast.2, f32[3,64,8192]{2,1,0:T(8,128)} %bitcast.3, f32[64,384]{1,0:T(8,128)} %q_hbm.1), custom_call_target="tpu_custom_call" | custom-call | tf_op jit(solution)/shard_map/dion/pallas_call | solution.py:760
  154.2 5.6 %outputs.1 = (f32[1,3,64,8192]{3,2,1,0:T(8,128)}, f32[3,64,8192]{2,1,0:T(8,128)}, f32[64,384]{1,0:T(8,128)}) custom-call(f32[3,4,4,4,2,64,128]{6,5,4,3,2,1,0:T(8,128)S(1)} %get-tuple-element.5.both_ref, f32[64,384]{1,0:T(8,128)S(1)} %get-tuple-element.6.basis_in), custom_call_target="tpu_custom_call" | custom-call | tf_op jit(solution)/shard_map/outputs/pallas_call | solution.py:784
